TPU v7x, 32 devices: a whole 2x2x4 slice. The times are simulated.
32 devices in a mesh: grp: 16 (over z, x, core), tp: 2 (over y).
Axes of the slice: x: 2, y: 2, z: 4, core: 2. Of those that a mesh axis runs over, the one named last changes fastest.
Arguments:
- tokens: bfloat16 [16, 1024, 2048], P(None, 'grp'), may hold values from -6 to 6
- w_query: bfloat16 [2048, 2048], P(None, 'tp'), may hold values from -0.375 to 0.375
- w_key: bfloat16 [2048, 2048], P(None, 'tp'), may hold values from -0.125 to 0.125
- w_value: bfloat16 [2048, 2048], P(None, 'tp'), may hold values from -0.125 to 0.125
- w_out: bfloat16 [2048, 2048], P('tp'), may hold values from -0.125 to 0.125
- own_cache: bfloat16 [16, 2, 2048, 2048], P('grp', None, None, 'tp'), may hold values from -330 to 330
- guest_cache: bfloat16 [16, 2, 2048, 2048], P('grp', None, None, 'tp'), may hold values from -6 to 6
- rec_hidden: bfloat16 [16, 256, 2048], P('grp'), may hold values from -6 to 6
- deal_order: int32 [16], replicated, may hold values from 0 to 15, each once
- own_len: int32 [16], replicated, may hold values from 256 to 2048, as said below
- guest_len: int32 [16], replicated, may hold values from 0 to 2048, as said below
- rec_index: int32 [16, 256], P('grp'), may hold values from 0 to 2047, as said below
Outputs:
- attn_out: bfloat16 [16, 1024, 2048], P(None, 'grp', 'tp')
Inputs may be any that keep to these rules, and one draw needn't show every extreme that they name: Rows 0 to own_len[g] - 1 of group g's own slot hold cached positions 0 to own_len[g] - 1 of the request served at group g; a request whose cache continues in a guest region fills its own slot. The guest_len[g] used rows of group g's guest region continue the cache of the request served at group (g + 8) mod 16. rec_index[g] holds 256 distinct rows of group g's own slot, each below own_len[g].
All inputs are finite; a program needn't handle non-finite values.
Results may differ from a plain program's by a relative error of at most 0.02.
The roundings to bfloat16 on the way count: a program that leaves them out, or rounds other values in their place, can miss the bound.
Values may be sent and summed in bfloat16 or wider, within the bound.
No kernel may reach another device: no remote copies, remote signals or barrier semaphores. Data moves between devices by JAX's collectives and lax.ppermute only.
A program may use at most 192 MiB of HBM per device.

v0:
```python
import functools
import math

import jax
import jax.numpy as jnp
from jax import lax
from jax.experimental import pallas as pl
from jax.experimental.pallas import tpu as pltpu
from jax.sharding import PartitionSpec as P

HEAD_DIM = 128
KEY_BLOCK = 1024
ROW_BLOCK = 256
STATS = 128
PIECE = 256
VMEM_LIMIT = 60 * 1024 * 1024

rope_base = 10000.0
norm_eps = 1e-05
LOG2E = math.log2(math.e)
LOWEST = -1e30


def params():
    return pltpu.CompilerParams(vmem_limit_bytes=VMEM_LIMIT)


def layer_norm(token_rows):
    widened = token_rows.astype(jnp.float32)
    centred = widened - jnp.mean(widened, axis=-1, keepdims=True)
    variance = jnp.mean(centred * centred, axis=-1, keepdims=True)
    return centred * lax.rsqrt(variance + norm_eps)


def rope_tables(positions):
    half_dim = HEAD_DIM // 2
    frequency = jnp.exp(-jnp.log(rope_base) * jnp.arange(half_dim, dtype=jnp.float32) / half_dim)
    angles = positions.astype(jnp.float32)[:, None] * frequency[None, :]
    cosine = jnp.cos(angles)
    sine = jnp.sin(angles)
    return (
        jnp.concatenate([cosine, cosine], axis=-1),
        jnp.concatenate([-sine, sine], axis=-1),
    )


def deal_kernel(order_ref, tp_ref, x_ref, first_ref, second_ref, guest_ref):
    each, cut, _ = first_ref.shape
    start = pl.program_id(0) * each
    for at in range(each):
        normed = layer_norm(x_ref[order_ref[start + at]]).astype(jnp.bfloat16)
        first_ref[at] = normed[:cut]
        second_ref[at] = normed[cut:]
        guest_ref[at] = normed


def deal(tokens, deal_order, tp_index, piece):
    groups, _, width = tokens.shape
    each = 4
    steps = groups // each
    cut = piece // 2
    own = pl.BlockSpec((each, cut, width), lambda d, order, t: (d, 0, 0))
    guest = pl.BlockSpec((each, piece, width), lambda d, order, t: ((d + steps // 2) % steps, 0, 0))
    return pl.pallas_call(
        deal_kernel,
        grid_spec=pltpu.PrefetchScalarGridSpec(
            num_scalar_prefetch=2,
            grid=(steps,),
            in_specs=[pl.BlockSpec((groups, piece, width), lambda d, order, t: (0, t[0], 0))],
            out_specs=[own, own, guest],
        ),
        out_shape=[
            jax.ShapeDtypeStruct((groups, rows, width), jnp.bfloat16) for rows in (cut, cut, piece)
        ],
        compiler_params=params(),
        name="deal",
    )(deal_order, tp_index, tokens)


def project_kernel(turned, heads, sources, cut, tp_ref, *refs):
    if sources > 1:
        mine_ref, other_ref, cos_ref, sin_ref, *refs, x_ref = refs
        shards_in, rows_each, _ = mine_ref.shape

        @pl.when(pl.program_id(0) == 0)
        def _():
            t = tp_ref[0]
            for piece in range(rows_each // cut):
                rows = slice(piece * cut, (piece + 1) * cut)
                for shard in range(shards_in):
                    at = (piece * shards_in + shard) * 2
                    for part_ref, side in ((mine_ref, t), (other_ref, 1 - t)):
                        start = pl.multiple_of((at + side) * cut, cut)
                        x_ref[pl.ds(start, cut), :] = part_ref[shard, rows, :]
    else:
        x_ref, cos_ref, sin_ref, *refs = refs
    count = len(turned)
    step = min(512, x_ref.shape[0])
    for first in range(0, x_ref.shape[0], step):
        rows = slice(first, first + step)
        for w_ref, out_ref, turn in zip(refs[:count], refs[count:], turned):
            product = jnp.dot(x_ref[rows, :], w_ref[...], preferred_element_type=jnp.float32)
            if not turn:
                out_ref[rows, :] = product.astype(jnp.bfloat16)
                continue
            for head in range(heads):
                cut = slice(head * HEAD_DIM, (head + 1) * HEAD_DIM)
                part = product[:, cut]
                swapped = pltpu.roll(part, HEAD_DIM // 2, 1)
                out_ref[rows, cut] = (
                    part * cos_ref[rows, :] + swapped * sin_ref[rows, :]
                ).astype(jnp.bfloat16)


def project(x, cut, tp_index, tables, table_at, weights, turned):
    depth = x[0].shape[-1]
    rows = sum(math.prod(part.shape[:-1]) for part in x)
    width = weights[0].shape[1]
    block = min(256, width)
    table = pl.BlockSpec((rows, HEAD_DIM), lambda n, t: (table_at, 0))
    count = len(weights)
    return pl.pallas_call(
        functools.partial(project_kernel, turned, block // HEAD_DIM, len(x), cut),
        grid_spec=pltpu.PrefetchScalarGridSpec(
            num_scalar_prefetch=1,
            grid=(width // block,),
            in_specs=[pl.BlockSpec(part.shape, lambda n, t, r=part.ndim: (0,) * r) for part in x]
            + [table, table]
            + [pl.BlockSpec((depth, block), lambda n, t: (0, n))] * count,
            out_specs=[pl.BlockSpec((rows, block), lambda n, t: (0, n))] * count,
            scratch_shapes=[pltpu.VMEM((rows, depth), jnp.bfloat16)] if len(x) > 1 else [],
        ),
        out_shape=[jax.ShapeDtypeStruct((rows, width), jnp.bfloat16)] * count,
        compiler_params=params(),
        cost_estimate=pl.CostEstimate(
            flops=rows * depth * width,
            bytes_accessed=rows * depth,
            transcendentals=0,
        ),
        name="project",
    )(tp_index, *x, *tables, *weights)


def replace_kernel(block, index_ref, cache_ref, keys_ref, values_ref, out_ref):
    first = pl.program_id(1) * block
    count = index_ref.shape[1]

    def fill(fresh_ref):
        row = first + lax.broadcasted_iota(jnp.int32, (block, count), 0)
        hits = jnp.where(row == index_ref[...], 1.0, 0.0)
        picked = jnp.dot(
            hits.astype(jnp.bfloat16), fresh_ref[...], preferred_element_type=jnp.float32
        )
        is_hit = jnp.sum(hits, axis=1, keepdims=True) > 0.5
        out_ref[0] = jnp.where(is_hit, picked, cache_ref[0, 0].astype(jnp.float32)).astype(
            jnp.bfloat16
        )

    for which, fresh_ref in enumerate((keys_ref, values_ref)):
        pl.when(pl.program_id(0) == which)(functools.partial(fill, fresh_ref))


def replace_rows(cache, keys, values, rec_index):
    _, _, rows, width = cache.shape
    count = rec_index.shape[1]
    block = 512
    return pl.pallas_call(
        functools.partial(replace_kernel, block),
        grid=(2, rows // block),
        in_specs=[
            pl.BlockSpec((1, count), lambda c, r: (0, 0)),
            pl.BlockSpec((1, 1, block, width), lambda c, r: (0, c, r, 0)),
            pl.BlockSpec((count, width), lambda c, r: (0, 0)),
            pl.BlockSpec((count, width), lambda c, r: (0, 0)),
        ],
        out_specs=pl.BlockSpec((1, block, width), lambda c, r: (c, r, 0)),
        out_shape=jax.ShapeDtypeStruct((2, rows, width), jnp.bfloat16),
        compiler_params=params(),
        cost_estimate=pl.CostEstimate(
            flops=4 * rows * count * width, bytes_accessed=10 * rows * width, transcendentals=0
        ),
        name="replace_rows",
    )(rec_index, cache, keys, values)


def fold_keys(jobs, m_ref, acc_ref):
    scale = HEAD_DIM**-0.5 * LOG2E

    def scores_of(job):
        _, queries, keys, _ = job
        for key_block, mask in keys():
            for at in range(0, key_block.shape[0], PIECE):
                scores = lax.dot_general(
                    queries(),
                    key_block[at : at + PIECE],
                    (((1,), (1,)), ((), ())),
                    preferred_element_type=jnp.float32,
                )
                if mask is not None:
                    scores = jnp.where(mask[:, at : at + PIECE], scores, LOWEST)
                yield scores

    upcoming = list(scores_of(jobs[0]))
    for at, (place, _, _, values) in enumerate(jobs):
        scores = upcoming
        ahead = scores_of(jobs[at + 1]) if at + 1 < len(jobs) else iter(())
        upcoming = []
        old_max = m_ref[place]
        widest = functools.reduce(jnp.maximum, scores)
        new_max = jnp.maximum(old_max, jnp.max(widest, axis=1, keepdims=True))
        factor = jnp.exp2((old_max - new_max) * scale)
        shift = new_max * scale
        shift = jnp.concatenate([shift] * (PIECE // HEAD_DIM), axis=1)
        weights = []
        for part in scores:
            upcoming += [found for _, found in zip(range(1), ahead)]
            weights.append(jnp.exp2(part * scale - shift).astype(jnp.bfloat16))
        upcoming += list(ahead)
        seen = values()
        widened = jnp.concatenate([seen, jnp.ones(seen.shape, jnp.bfloat16)], axis=1)
        product = jnp.dot(
            jnp.concatenate(weights, axis=1), widened, preferred_element_type=jnp.float32
        )
        acc_ref[place] = acc_ref[place] * jnp.concatenate([factor, factor], axis=1) + product
        m_ref[place] = new_max


def attend_kernel(causal, chunk, chunks, piece, sides, count_ref, q_ref, k_ref, v_ref, *refs):
    if causal:
        new_refs, refs = refs[: 2 * chunks], refs[2 * chunks :]
    o_ref, lse_ref, m_ref, acc_ref = refs
    scale = HEAD_DIM**-0.5 * LOG2E
    rows_in = q_ref.shape[0]
    per_step = q_ref.shape[1] // HEAD_DIM
    step = pl.program_id(0)
    used = count_ref[0]
    blocks = [slice(at, at + ROW_BLOCK) for at in range(0, rows_in, ROW_BLOCK)]
    places = [(head, block) for head in range(per_step) for block in blocks]
    m_ref[...] = jnp.full(m_ref.shape, LOWEST, jnp.float32)
    acc_ref[...] = jnp.zeros(acc_ref.shape, jnp.float32)
    k_all = k_ref.at[(0,) * (len(k_ref.shape) - 2)]
    v_all = v_ref.at[(0,) * (len(v_ref.shape) - 2)]

    def head_cut(head):
        return slice(head * HEAD_DIM, (head + 1) * HEAD_DIM)

    def job(place, picks):
        head, block = place
        cut = head_cut(head)

        def values():
            found = [values_ref[at, cut] for _, values_ref, at, _ in picks]
            return found[0] if len(found) == 1 else jnp.concatenate(found, axis=0)

        return (
            place,
            lambda: q_ref[block, cut],
            lambda: [(keys_ref[at, cut], mask) for keys_ref, _, at, mask in picks],
            values,
        )

    def visit(block, masked):
        start = pl.multiple_of(block * KEY_BLOCK, KEY_BLOCK)
        mask = None
        if masked:
            mask = lax.broadcasted_iota(jnp.int32, (1, KEY_BLOCK), 1) < used - start
        picks = [(k_all, v_all, pl.ds(start, KEY_BLOCK), mask)]
        fold_keys([job(place, picks) for place in places], m_ref, acc_ref)

    full = used // KEY_BLOCK
    pl.loop(0, full)(lambda block: visit(block, False))

    @pl.when(used % KEY_BLOCK > 0)
    def _():
        visit(full, True)

    if causal:
        each = piece // sides
        row = lax.broadcasted_iota(jnp.int32, (ROW_BLOCK, ROW_BLOCK), 0)
        key = lax.broadcasted_iota(jnp.int32, (ROW_BLOCK, ROW_BLOCK), 1)

        def natural(at, of_chunk):
            within = at % piece
            inside = (within // each) * (each * chunks) + of_chunk * each + within % each
            return (at // piece) * (piece * chunks) + inside

        row_at = natural(row, chunk)
        masks = [natural(key, key_chunk) <= row_at for key_chunk in range(chunks)]
        jobs = []
        for place in places:
            picks = []
            for key_chunk in range(chunks):
                pair = new_refs[2 * key_chunk : 2 * key_chunk + 2]
                if place[1].start:
                    picks.append((*pair, slice(0, place[1].start), None))
                picks.append((*pair, place[1], masks[key_chunk]))
            jobs.append(job(place, picks))
        fold_keys(jobs, m_ref, acc_ref)

    for head, block in places:
        rows = block
        total = acc_ref[head, block, HEAD_DIM:]
        seen = total > 0.0
        safe = jnp.where(seen, total, 1.0)
        out = (acc_ref[head, block, :HEAD_DIM] / safe).astype(jnp.bfloat16)
        column = step * per_step + head
        o_ref[rows, pl.ds(pl.multiple_of(column * HEAD_DIM, HEAD_DIM), HEAD_DIM)] = out
        lse = jnp.where(seen, m_ref[head, block] * scale + jnp.log2(safe), LOWEST)
        lane = lax.broadcasted_iota(jnp.int32, (ROW_BLOCK, STATS), 1)
        before = jnp.where(column == 0, 0.0, lse_ref[rows, :])
        lse_ref[rows, :] = jnp.where(lane == column, lse, before)

    @pl.when(step == pl.num_programs(0) - 1)
    def _():
        for rows in blocks:
            left = lse_ref[rows, :]
            packed = jnp.zeros_like(left)
            for turn in range(3):
                part = left.astype(jnp.bfloat16).astype(jnp.float32)
                left = left - part
                packed = packed + (pltpu.roll(part, turn * STATS // 4, 1) if turn else part)
            o_ref[rows, o_ref.shape[1] - STATS :] = packed.astype(jnp.bfloat16)


def attend(count, rows_in, groups, chunk, chunks, sides, query, cache, new=()):
    queries, q_at = query
    width = queries.shape[1]
    heads = width // HEAD_DIM
    per_step = 2
    rows = cache.shape[-2]
    causal = len(new) > 0
    lead = cache.ndim - 3
    shape = (1,) * (lead + 1) + (rows, per_step * HEAD_DIM)
    every = pl.BlockSpec((rows_in, per_step * HEAD_DIM), lambda h, n: (0, h))

    def half(which):
        return pl.BlockSpec(shape, lambda h, n: (0,) * lead + (which, 0, h))

    keys_seen = rows + (rows_in if causal else 0)
    out = pl.pallas_call(
        functools.partial(attend_kernel, causal, chunk, chunks, rows_in // groups, sides),
        grid_spec=pltpu.PrefetchScalarGridSpec(
            num_scalar_prefetch=1,
            grid=(heads // per_step,),
            in_specs=[
                pl.BlockSpec((rows_in, per_step * HEAD_DIM), lambda h, n: (q_at, h)),
                half(0),
                half(1),
            ]
            + [every] * len(new),
            out_specs=pl.BlockSpec((rows_in, width + STATS), lambda h, n: (0, 0)),
            scratch_shapes=[
                pltpu.VMEM((rows_in, STATS), jnp.float32),
                pltpu.VMEM((per_step, rows_in, HEAD_DIM), jnp.float32),
                pltpu.VMEM((per_step, rows_in, 2 * HEAD_DIM), jnp.float32),
            ],
        ),
        out_shape=jax.ShapeDtypeStruct((rows_in, width + STATS), jnp.bfloat16),
        compiler_params=params(),
        cost_estimate=pl.CostEstimate(
            flops=2 * rows_in * keys_seen * width,
            bytes_accessed=4 * rows_in * width,
            transcendentals=0,
        ),
        name="attend_own" if causal else "attend_guest",
    )(count, queries, cache, cache, *new)
    return out.reshape(groups, rows_in // groups, width + STATS)


def merge_kernel(groups, heads, inverse_ref, tp_ref, own_ref, guest_ref, w_ref, *refs):
    *out_refs, att_ref, share_ref = refs
    piece = own_ref.shape[1]
    width = heads * HEAD_DIM
    step = pl.program_id(0)

    def stats(part_ref, at):
        packed = part_ref[at, :, width:].astype(jnp.float32)
        return (
            packed
            + pltpu.roll(packed, STATS - STATS // 4, 1)
            + pltpu.roll(packed, STATS - STATS // 2, 1)
        )

    @pl.when(step == 0)
    def _():
        lane = lax.broadcasted_iota(jnp.int32, (piece, STATS), 1)
        rows = [pl.ds(request * piece, piece) for request in range(groups)]
        for request in range(groups):
            source = inverse_ref[request]
            helper = lax.rem(source + groups // 2, groups)
            ahead = stats(guest_ref, helper) - stats(own_ref, source)
            share = jnp.where(lane < heads, 1.0 / (1.0 + jnp.exp2(ahead)), 0.0)
            high = share.astype(jnp.bfloat16).astype(jnp.float32)
            rest = pltpu.roll(share - high, STATS // 4, 1)
            share_ref[rows[request], :] = (high + rest).astype(jnp.bfloat16)
        lane = lax.broadcasted_iota(jnp.int32, (STATS, width), 0)
        head = lax.broadcasted_iota(jnp.int32, (STATS, width), 1) // HEAD_DIM
        spread = jnp.where((lane == head) | (lane == head + STATS // 4), 1.0, 0.0)
        shares = jnp.dot(
            share_ref[...], spread.astype(jnp.bfloat16), preferred_element_type=jnp.float32
        )
        for request in range(groups):
            source = inverse_ref[request]
            helper = lax.rem(source + groups // 2, groups)
            own = own_ref[source, :, :width].astype(jnp.float32)
            guest = guest_ref[helper, :, :width].astype(jnp.float32)
            share = shares[request * piece : (request + 1) * piece]
            att_ref[rows[request], :] = (guest + share * (own - guest)).astype(jnp.bfloat16)

    product = jnp.dot(att_ref[...], w_ref[...], preferred_element_type=jnp.float32).astype(
        jnp.bfloat16
    )
    each = pl.num_programs(0) // len(out_refs)
    for at, out_ref in enumerate(out_refs):
        pl.when(step // each == at)(functools.partial(out_ref.__setitem__, ..., product))


def merge(inverse, tp_index, splits, own, guest, w_out):
    groups, piece, _ = guest.shape
    width = w_out.shape[0]
    heads = width // HEAD_DIM
    columns = w_out.shape[1]
    block = 512
    rows = groups * piece
    steps = columns // block
    each = steps // splits

    def w_at(n, i, t):
        return (0, (n + each * (1 - t[0])) % steps if splits == 2 else n)

    def out_at(which):
        return lambda n, i, t: (0, jnp.clip(n - which * each, 0, each - 1))

    part = pl.BlockSpec(guest.shape, lambda n, i, t: (0, 0, 0))
    return pl.pallas_call(
        functools.partial(merge_kernel, groups, heads),
        grid_spec=pltpu.PrefetchScalarGridSpec(
            num_scalar_prefetch=2,
            grid=(steps,),
            in_specs=[part, part, pl.BlockSpec((width, block), w_at)],
            out_specs=[pl.BlockSpec((rows, block), out_at(which)) for which in range(splits)],
            scratch_shapes=[
                pltpu.VMEM((rows, width), jnp.bfloat16),
                pltpu.VMEM((rows, STATS), jnp.bfloat16),
            ],
        ),
        out_shape=[jax.ShapeDtypeStruct((rows, columns // splits), jnp.bfloat16)] * splits,
        compiler_params=params(),
        cost_estimate=pl.CostEstimate(
            flops=rows * width * columns,
            bytes_accessed=rows * columns,
            transcendentals=0,
        ),
        name="merge",
    )(inverse, tp_index, own, guest, w_out)


def exchange(value):
    return lax.all_to_all(value, "grp", split_axis=0, concat_axis=0, tiled=True)


def shards(
    tokens,
    w_query,
    w_key,
    w_value,
    w_out,
    own_cache,
    guest_cache,
    rec_hidden,
    deal_order,
    own_len,
    guest_len,
    rec_index,
):
    groups = lax.axis_size("grp")
    tp_size = lax.axis_size("tp")
    group_id = lax.axis_index("grp")
    tp_id = lax.axis_index("tp")
    partner_id = (group_id + groups // 2) % groups
    width = w_query.shape[1]
    heads = width // HEAD_DIM
    shard_rows = tokens.shape[1]
    span = shard_rows * groups
    piece = shard_rows // tp_size

    chunks = 2
    chunk_rows = shard_rows // chunks
    paired = tp_size == 2 and piece % 32 == 0
    sides = 2 if paired else 1
    each = chunk_rows // sides
    tp_index = tp_id.astype(jnp.int32)[None]
    tied = lax.optimization_barrier
    neighbour = [(0, 1), (1, 0)]

    if paired:
        dealt = deal(tokens, deal_order, tp_index, piece)
        own_rows, guest_rows = dealt[:2], dealt[2]
    else:
        mine = lax.dynamic_slice_in_dim(tokens, tp_id * piece, piece, 1)
        normed = layer_norm(mine).astype(jnp.bfloat16)
        own_rows = jnp.take(normed, deal_order, axis=0)
        guest_rows = jnp.roll(own_rows, groups // 2, axis=0)

    def in_chunks(rows):
        rows = rows.reshape(groups, sides, chunks, each, -1)
        return jnp.transpose(rows, (2, 0, 1, 3, 4)).reshape(chunks, span // chunks, -1)

    def with_other(arrived):
        return [arrived, lax.ppermute(arrived, "tp", neighbour)]

    def gathered(rows):
        arrived = lax.all_gather(exchange(rows), "tp", axis=0)
        parts = in_chunks(jnp.transpose(arrived, (1, 0, 2, 3)))
        return [[part] for part in parts]

    row_order = in_chunks(jnp.arange(span, dtype=jnp.int32)).reshape(span)

    def place(owner, helper):
        return own_len[owner] + guest_len[helper] + row_order

    def projected(x, tables, chunk, weights, turned):
        return project(x, each, tp_index, tables, chunk, weights, turned)

    def own_project(chunk):
        return projected(
            own_x[chunk], own_tables, chunk, (w_query, w_key, w_value), (True, True, False)
        )

    def own_attend(chunk, queries):
        count = own_len[group_id][None]
        rows_in = span // chunks
        return attend(count, rows_in, groups, chunk, chunks, sides, (queries, 0), cache, new)

    def guest_attend(chunk, query):
        count = guest_len[group_id][None]
        rows_in = span // chunks
        return attend(count, rows_in, groups, chunk, chunks, sides, query, guest_cache)

    def guest_project():
        if paired:
            (queries,) = projected(guest_x, guest_tables, 0, (w_query,), (True,))
            return [(queries, 0), (queries, 1)]
        return [
            (projected(guest_x[chunk], guest_tables, chunk, (w_query,), (True,))[0], 0)
            for chunk in range(chunks)
        ]

    own_tables = rope_tables(place(group_id, partner_id))
    guest_tables = rope_tables(place(partner_id, group_id))
    rec_tables = rope_tables(rec_index[0])
    rec_rows = layer_norm(rec_hidden[0]).astype(jnp.bfloat16)
    rec_parts = projected((rec_rows,), rec_tables, 0, (w_key, w_value), (True, False))

    if paired:
        arrived = exchange(own_rows[0])
        arrived, own_tables, guest_tables, rec_parts, own_rows = tied(
            (arrived, own_tables, guest_tables, rec_parts, own_rows)
        )
        own_x = [with_other(arrived)]
        cache = replace_rows(own_cache, *rec_parts, rec_index)
        arrived = exchange(own_rows[1])
        arrived, cache, own_x, guest_rows = tied((arrived, cache, own_x, guest_rows))
        own_x.append(with_other(arrived))
        arrived = exchange(guest_rows)
        made = [own_project(chunk) for chunk in range(chunks)]
        arrived, made = tied((arrived, made))
        guest_x = with_other(arrived)
    else:
        cache = replace_rows(own_cache, *rec_parts, rec_index)
        own_x = gathered(own_rows)
        guest_x = gathered(guest_rows)
        made = [own_project(chunk) for chunk in range(chunks)]
    new = [part for parts in made for part in parts[1:]]
    inverse = jnp.sum(
        jnp.where(
            deal_order[None, :] == jnp.arange(groups, dtype=deal_order.dtype)[:, None],
            jnp.arange(groups, dtype=jnp.int32)[None, :],
            0,
        ),
        axis=1,
    )

    own_out = [own_attend(0, made[0][0])]
    own_out, query = tied((own_out, made[1][0]))
    own_part = [exchange(own_out[0])]
    own_out.append(own_attend(1, query))
    own_part, own_out = tied((own_part, own_out))
    own_part.append(exchange(own_out[1]))
    guest_x, own_out = tied((guest_x, own_out))
    queries = guest_project()
    guest_out = [guest_attend(0, queries[0])]
    own_part, guest_out, query = tied((own_part, guest_out, queries[1][0]))
    guest_part = [exchange(guest_out[0])]
    guest_out.append(guest_attend(1, (query, queries[1][1])))
    guest_part, guest_out = tied((guest_part, guest_out))
    guest_part.append(exchange(guest_out[1]))

    def merged(chunk):
        splits = 2 if paired and chunk else 1
        return merge(inverse, tp_index, splits, own_part[chunk], guest_part[chunk], w_out)

    def summed(partial, split):
        if split:
            theirs, mine = partial
            arrived = lax.ppermute(theirs, "tp", neighbour).astype(jnp.float32)
            total = (mine.astype(jnp.float32) + arrived).astype(jnp.bfloat16)
        else:
            total = lax.psum_scatter(partial[0], "tp", scatter_dimension=1, tiled=True)
        return total.reshape(groups, sides, 1, each, -1)

    partial = merged(0)
    guest_part[1], partial = tied((guest_part[1], partial))
    mixed = [summed(partial, False), summed(merged(1), paired)]
    return jnp.concatenate(mixed, axis=2).reshape(groups, shard_rows, -1)


def solution(mesh):
    return jax.shard_map(
        shards,
        mesh=mesh,
        in_specs=(
            P(None, "grp", None),
            P(None, "tp"),
            P(None, "tp"),
            P(None, "tp"),
            P("tp", None),
            P("grp", None, None, "tp"),
            P("grp", None, None, "tp"),
            P("grp", None, None),
            P(),
            P(),
            P(),
            P("grp", None),
        ),
        out_specs=P(None, "grp", "tp"),
        check_vma=False,
    )
```

profile of v0, /device:TPU:0, one launch (start us, length us, event | category | flops | bytes accessed | tf_op | source)
XLA Modules:
  0.0 363.4 jit_solution(12117861363061025927)
XLA Ops:
  6.5 5.3 %deal.1 = (bf16[16,16,2048]{2,1,0:T(8,128)(2,1)}, bf16[16,16,2048]{2,1,0:T(8,128)(2,1)}, bf16[16,32,2048]{2,1,0:T(8,128)(2,1)}) custom-call(s32[16]{0:T(128)} %order_ref.1, s32[1]{0:T(128)} %bitcast.tp_ref, bf16[16,64,2048]{2,1,0:T(8,128)(2,1)} %x_ref.1), custom_call_target="tpu_custom_call" | custom-call | tf_op jit(solution)/shard_map/deal/pallas_call | solution.py:64
  11.8 7.5 %all-to-all-start = ((bf16[16,16,2048]{2,1,0:T(8,128)(2,1)}), bf16[16,16,2048]{2,1,0:T(8,128)(2,1)S(1)}, u32[]{:S(2)}, u32[]{:S(2)}) async-start(bf16[16,16,2048]{2,1,0:T(8,128)(2,1)} %get-tuple-element.52), calls=%async_computation | async-start | bytes 2097152 | tf_op jit(solution)/shard_map/all_to_all | solution.py:459
  26.1 6.8 %project.4 = (bf16[256,1024]{1,0:T(8,128)(2,1)}, bf16[256,1024]{1,0:T(8,128)(2,1)}) custom-call(s32[1]{0:T(128)} %bitcast.tp_ref, bf16[256,2048]{1,0:T(8,128)(2,1)} %fusion.4.refs_0_, f32[256,128]{1,0:T(8,128)} %get-tuple-element.117.refs_1_, f32[256,128]{1,0:T(8,128)} %get-tuple-element.118.refs_2_, bf16[2048,1024]{1,0:T(8,128)(2,1)} %refs_5_.3, ...), custom_call_target="tpu_custom_call" | custom-call | flops 536870912 | bytes 524288 | tf_op jit(solution)/shard_map/project/pallas_call | solution.py:122
  32.9 3.7 %fusion.6 = (f32[1024,64]{1,0:T(8,128)S(1)}, f32[1024,64]{1,0:T(8,128)S(1)}, f32[1024,64]{1,0:T(8,128)S(1)}, f32[1024,64]{1,0:T(8,128)S(1)}, f32[1024,64]{1,0:T(8,128)S(1)}, /*index=5*/f32[1024,64]{1,0:T(8,128)S(1)}) fusion(f32[64]{0:T(128)S(1)} %multiply_exponential_fusion, f32[1024]{0:T(1024)S(1)} %convert_element_type.59, f32[1024]{0:T(1024)S(1)} %convert_element_type.56), kind=kLoop, calls=%fused_computation.20 | loop fusion | flops 262144 | bytes 1581312 | tf_op jit(solution)/shard_map/neg | solution.py:43
  40.7 1.6 all-to-all-done.refs_0_
  42.3 6.9 %all-to-all-start.1 = ((bf16[16,16,2048]{2,1,0:T(8,128)(2,1)}), bf16[16,16,2048]{2,1,0:T(8,128)(2,1)S(1)}, u32[]{:S(2)}, u32[]{:S(2)}) async-start(bf16[16,16,2048]{2,1,0:T(8,128)(2,1)} %get-tuple-element.56), calls=%async_computation.1 | async-start | bytes 2097152 | tf_op jit(solution)/shard_map/all_to_all | solution.py:459
  49.1 1.6 collective-permute-start
  50.7 10.9 %replace_rows.1.k_ref.v_ref = bf16[2,2048,1024]{2,1,0:T(8,128)(2,1)} custom-call(s32[1,256]{1,0:T(1,128)} %index_ref.1, bf16[1,2,2048,1024]{3,2,1,0:T(8,128)(2,1)} %cache_ref.1, bf16[256,1024]{1,0:T(8,128)(2,1)} %get-tuple-element.57.keys_ref, bf16[256,1024]{1,0:T(8,128)(2,1)} %get-tuple-element.58.values_ref), custom_call_target="tpu_custom_call" | custom-call | flops 2147483648 | bytes 20971520 | tf_op jit(solution)/shard_map/replace_rows/pallas_call | solution.py:167
  61.6 13.0 %collective-permute-done.refs_1_ = bf16[16,16,2048]{2,1,0:T(8,128)(2,1)S(1)} collective-permute-done((bf16[16,16,2048]{2,1,0:T(8,128)(2,1)S(1)}, bf16[16,16,2048]{2,1,0:T(8,128)(2,1)S(1)}, u32[]{:S(2)}, u32[]{:S(2)}) %collective-permute-start) | collective-permute-done | bytes 1048608 | tf_op jit(solution)/shard_map/ppermute | solution.py:510
  75.9 5.8 %all-to-all-start.2 = ((bf16[16,32,2048]{2,1,0:T(8,128)(2,1)}), bf16[16,32,2048]{2,1,0:T(8,128)(2,1)S(1)}, u32[]{:S(2)}, u32[]{:S(2)}) async-start(bf16[16,32,2048]{2,1,0:T(8,128)(2,1)} %get-tuple-element.61), calls=%async_computation.2 | async-start | bytes 4194304 | tf_op jit(solution)/shard_map/all_to_all | solution.py:459
  81.7 1.6 collective-permute-start.1
  83.3 11.7 %project.5 = (bf16[512,1024]{1,0:T(8,128)(2,1)}, bf16[512,1024]{1,0:T(8,128)(2,1)}, bf16[512,1024]{1,0:T(8,128)(2,1)}) custom-call(s32[1]{0:T(128)} %bitcast.tp_ref, bf16[16,16,2048]{2,1,0:T(8,128)(2,1)} %copy-done.5, bf16[16,16,2048]{2,1,0:T(8,128)(2,1)} %copy-done.7, f32[1024,128]{1,0:T(8,128)} %pad_maximum_fusion.1.refs_2_, ...), custom_call_target="tpu_custom_call" | custom-call | flops 1073741824 | bytes 1048576 | tf_op jit(solution)/shard_map/project/pallas_call | solution.py:122
  95.0 12.4 %collective-permute-done.1.refs_1_ = bf16[16,16,2048]{2,1,0:T(8,128)(2,1)S(1)} collective-permute-done((bf16[16,16,2048]{2,1,0:T(8,128)(2,1)}, bf16[16,16,2048]{2,1,0:T(8,128)(2,1)S(1)}, u32[]{:S(2)}, u32[]{:S(2)}) %collective-permute-start.1) | collective-permute-done | bytes 1048608 | tf_op jit(solution)/shard_map/ppermute | solution.py:510
  108.5 11.8 %project.6 = (bf16[512,1024]{1,0:T(8,128)(2,1)}, bf16[512,1024]{1,0:T(8,128)(2,1)}, bf16[512,1024]{1,0:T(8,128)(2,1)}) custom-call(s32[1]{0:T(128)} %bitcast.tp_ref, bf16[16,16,2048]{2,1,0:T(8,128)(2,1)} %copy-done.6, bf16[16,16,2048]{2,1,0:T(8,128)(2,1)} %copy-done.8, f32[1024,128]{1,0:T(8,128)} %pad_maximum_fusion.1.refs_2_, ...), custom_call_target="tpu_custom_call" | custom-call | flops 1073741824 | bytes 1048576 | tf_op jit(solution)/shard_map/project/pallas_call | solution.py:122
  120.2 2.6 all-to-all-done.2.refs_0_
  122.8 22.6 %attend_own.2 = bf16[512,1152]{1,0:T(8,128)(2,1)} custom-call(s32[1]{0:T(128)} %get-tuple-element.115.count_ref, bf16[512,1024]{1,0:T(8,128)(2,1)} %get-tuple-element.73.q_ref, bf16[2,2048,1024]{2,1,0:T(8,128)(2,1)} %replace_rows.1.k_ref.v_ref, bf16[2,2048,1024]{2,1,0:T(8,128)(2,1)} %replace_rows.1.k_ref.v_ref, bf16[512,1024]{1,0:T(8,128)(2,1)} %get-tuple-element.75.refs_0_, ...), custom_call_target="tpu_custom_call" | custom-call | flops 2684354560 | bytes 2097152 | tf_op jit(solution)/shard_map/attend_own/pallas_call | solution.py:340
  145.5 11.6 %all-to-all-start.3 = ((bf16[16,32,1152]{2,1,0:T(8,128)(2,1)}), bf16[16,32,1152]{2,1,0:T(8,128)(2,1)S(1)}, u32[]{:S(2)}, u32[]{:S(2)}) async-start(bf16[16,32,1152]{2,1,0:T(8,128)(2,1)} %bitcast.33), calls=%async_computation.3 | async-start | bytes 2359296 | tf_op jit(solution)/shard_map/all_to_all | solution.py:459
  157.1 1.6 collective-permute-start.2
  158.7 22.5 %attend_own.3 = bf16[512,1152]{1,0:T(8,128)(2,1)} custom-call(s32[1]{0:T(128)} %get-tuple-element.115.count_ref, bf16[512,1024]{1,0:T(8,128)(2,1)} %get-tuple-element.81.q_ref, bf16[2,2048,1024]{2,1,0:T(8,128)(2,1)} %replace_rows.1.k_ref.v_ref, bf16[2,2048,1024]{2,1,0:T(8,128)(2,1)} %replace_rows.1.k_ref.v_ref, bf16[512,1024]{1,0:T(8,128)(2,1)} %get-tuple-element.75.refs_0_, ...), custom_call_target="tpu_custom_call" | custom-call | flops 2684354560 | bytes 2097152 | tf_op jit(solution)/shard_map/attend_own/pallas_call | solution.py:340
  182.2 7.5 %all-to-all-start.4 = ((bf16[16,32,1152]{2,1,0:T(8,128)(2,1)}), bf16[16,32,1152]{2,1,0:T(8,128)(2,1)}, u32[]{:S(2)}, u32[]{:S(2)}) async-start(bf16[16,32,1152]{2,1,0:T(8,128)(2,1)} %bitcast.31), calls=%async_computation.4 | async-start | bytes 2359296 | tf_op jit(solution)/shard_map/all_to_all | solution.py:459
  189.7 15.5 %collective-permute-done.2.refs_1_ = bf16[16,32,2048]{2,1,0:T(8,128)(2,1)} collective-permute-done((bf16[16,32,2048]{2,1,0:T(8,128)(2,1)S(1)}, bf16[16,32,2048]{2,1,0:T(8,128)(2,1)}, u32[]{:S(2)}, u32[]{:S(2)}) %collective-permute-start.2) | collective-permute-done | bytes 2097184 | tf_op jit(solution)/shard_map/ppermute | solution.py:510
  205.2 9.8 %project.7.q_ref = bf16[1024,1024]{1,0:T(8,128)(2,1)} custom-call(s32[1]{0:T(128)} %bitcast.tp_ref, bf16[16,32,2048]{2,1,0:T(8,128)(2,1)} %copy-done.1, bf16[16,32,2048]{2,1,0:T(8,128)(2,1)} %collective-permute-done.2.refs_1_, f32[1024,128]{1,0:T(8,128)} %pad_maximum_fusion.3.refs_2_, f32[1024,128]{1,0:T(8,128)} %pad_maximum_fusion.4.refs_3_, ...), custom_call_target="tpu_custom_call" | custom-call | flops 2147483648 | bytes 2097152 | tf_op jit(solution)/shard_map/project/pallas_call | solution.py:122
  215.0 17.2 %attend_guest.2 = bf16[512,1152]{1,0:T(8,128)(2,1)} custom-call(s32[1]{0:T(128)} %get-tuple-element.111.count_ref, bf16[1024,1024]{1,0:T(8,128)(2,1)} %project.7.q_ref, bf16[1,2,2048,1024]{3,2,1,0:T(8,128)(2,1)} %v_ref.3, bf16[1,2,2048,1024]{3,2,1,0:T(8,128)(2,1)} %v_ref.3), custom_call_target="tpu_custom_call" | custom-call | flops 2147483648 | bytes 2097152 | tf_op jit(solution)/shard_map/attend_guest/pallas_call | solution.py:340
  232.2 6.1 %all-to-all-start.5 = ((bf16[16,32,1152]{2,1,0:T(8,128)(2,1)}), bf16[16,32,1152]{2,1,0:T(8,128)(2,1)S(1)}, u32[]{:S(2)}, u32[]{:S(2)}) async-start(bf16[16,32,1152]{2,1,0:T(8,128)(2,1)} %bitcast.34), calls=%async_computation.5 | async-start | bytes 2359296 | tf_op jit(solution)/shard_map/all_to_all | solution.py:459
  238.3 17.2 %attend_guest.3 = bf16[512,1152]{1,0:T(8,128)(2,1)} custom-call(s32[1]{0:T(128)} %get-tuple-element.111.count_ref, bf16[1024,1024]{1,0:T(8,128)(2,1)} %project.7.q_ref, bf16[1,2,2048,1024]{3,2,1,0:T(8,128)(2,1)} %v_ref.3, bf16[1,2,2048,1024]{3,2,1,0:T(8,128)(2,1)} %v_ref.3), custom_call_target="tpu_custom_call" | custom-call | flops 2147483648 | bytes 2097152 | tf_op jit(solution)/shard_map/attend_guest/pallas_call | solution.py:340
  255.5 7.9 %all-to-all-done.5.guest_ref = bf16[16,32,1152]{2,1,0:T(8,128)(2,1)S(1)} async-done(((bf16[16,32,1152]{2,1,0:T(8,128)(2,1)}), bf16[16,32,1152]{2,1,0:T(8,128)(2,1)S(1)}, u32[]{:S(2)}, u32[]{:S(2)}) %all-to-all-start.5) | async-done | bytes 1179680 | tf_op jit(solution)/shard_map/all_to_all | solution.py:459
  263.4 7.5 %all-to-all-start.6 = ((bf16[16,32,1152]{2,1,0:T(8,128)(2,1)}), bf16[16,32,1152]{2,1,0:T(8,128)(2,1)S(1)}, u32[]{:S(2)}, u32[]{:S(2)}) async-start(bf16[16,32,1152]{2,1,0:T(8,128)(2,1)} %bitcast.32), calls=%async_computation.6 | async-start | bytes 2359296 | tf_op jit(solution)/shard_map/all_to_all | solution.py:459
  271.6 8.0 %merge.2 = bf16[512,2048]{1,0:T(8,128)(2,1)} custom-call(s32[16]{0:T(128)} %select_reduce_fusion.inverse_ref, s32[1]{0:T(128)} %bitcast.tp_ref, bf16[16,32,1152]{2,1,0:T(8,128)(2,1)} %copy-done.2, bf16[16,32,1152]{2,1,0:T(8,128)(2,1)} %copy-done.3, bf16[1024,2048]{1,0:T(8,128)(2,1)} %w_ref.3), custom_call_target="tpu_custom_call" | custom-call | flops 1073741824 | bytes 1048576 | tf_op jit(solution)/shard_map/merge/pallas_call | solution.py:435
  279.7 16.4 %all-to-all-done.6.guest_ref = bf16[16,32,1152]{2,1,0:T(8,128)(2,1)S(1)} async-done(((bf16[16,32,1152]{2,1,0:T(8,128)(2,1)}), bf16[16,32,1152]{2,1,0:T(8,128)(2,1)S(1)}, u32[]{:S(2)}, u32[]{:S(2)}) %all-to-all-start.6) | async-done | bytes 1179680 | tf_op jit(solution)/shard_map/all_to_all | solution.py:459
  297.1 8.3 %merge.3 = (bf16[512,1024]{1,0:T(8,128)(2,1)}, bf16[512,1024]{1,0:T(8,128)(2,1)}) custom-call(s32[16]{0:T(128)} %select_reduce_fusion.inverse_ref, s32[1]{0:T(128)} %bitcast.tp_ref, bf16[16,32,1152]{2,1,0:T(8,128)(2,1)} %all-to-all-done.4.own_ref, bf16[16,32,1152]{2,1,0:T(8,128)(2,1)} %copy-done.4, bf16[1024,2048]{1,0:T(8,128)(2,1)} %w_ref.3), custom_call_target="tpu_custom_call" | custom-call | flops 1073741824 | bytes 1048576 | tf_op jit(solution)/shard_map/merge/pallas_call | solution.py:435
  306.9 45.0 %collective-permute-done.3 = bf16[512,1024]{1,0:T(8,128)(2,1)S(1)} collective-permute-done((bf16[512,1024]{1,0:T(8,128)(2,1)}, bf16[512,1024]{1,0:T(8,128)(2,1)S(1)}, u32[]{:S(2)}, u32[]{:S(2)}) %collective-permute-start.3) | collective-permute-done | bytes 1048608 | tf_op jit(solution)/shard_map/ppermute | solution.py:606
  352.0 1.6 add_convert_fusion
  (54 shorter events, 17.8 us)
Async XLA Ops:
  11.8 7.6 %copy-start.10 = (s32[16]{0:T(128)S(1)}, s32[16]{0:T(128)}, u32[]{:S(2)}) copy-start(s32[16]{0:T(128)} %param.22) | copy-start | bytes 196
  11.8 7.6 %copy-start.11 = (s32[16]{0:T(128)S(1)}, s32[16]{0:T(128)}, u32[]{:S(2)}) copy-start(s32[16]{0:T(128)} %param.21) | copy-start | bytes 196
  11.8 11.0 %copy-start.9 = (s32[1,256]{1,0:T(1,128)S(1)}, s32[1,256]{1,0:T(1,128)}, u32[]{:S(2)}) copy-start(s32[1,256]{1,0:T(1,128)} %index_ref.1) | copy-start | bytes 3076
  11.8 11.0 %copy-start = (bf16[1,256,2048]{2,1,0:T(8,128)(2,1)S(1)}, bf16[1,256,2048]{2,1,0:T(8,128)(2,1)}, u32[]{:S(2)}) copy-start(bf16[1,256,2048]{2,1,0:T(8,128)(2,1)} %param.19) | copy-start | bytes 3145732
  11.8 30.5 %all-to-all-start = ((bf16[16,16,2048]{2,1,0:T(8,128)(2,1)}), bf16[16,16,2048]{2,1,0:T(8,128)(2,1)S(1)}, u32[]{:S(2)}, u32[]{:S(2)}) async-start(bf16[16,16,2048]{2,1,0:T(8,128)(2,1)} %get-tuple-element.52), calls=%async_computation | async-start | bytes 2097152 | tf_op jit(solution)/shard_map/all_to_all | solution.py:459
  42.3 19.3 %copy-start.5 = (bf16[16,16,2048]{2,1,0:T(8,128)(2,1)}, bf16[16,16,2048]{2,1,0:T(8,128)(2,1)S(1)}, u32[]{:S(2)}) copy-start(bf16[16,16,2048]{2,1,0:T(8,128)(2,1)S(1)} %all-to-all-done.refs_0_) | copy-start | bytes 3145732
  42.3 32.4 %all-to-all-start.1 = ((bf16[16,16,2048]{2,1,0:T(8,128)(2,1)}), bf16[16,16,2048]{2,1,0:T(8,128)(2,1)S(1)}, u32[]{:S(2)}, u32[]{:S(2)}) async-start(bf16[16,16,2048]{2,1,0:T(8,128)(2,1)} %get-tuple-element.56), calls=%async_computation.1 | async-start | bytes 2097152 | tf_op jit(solution)/shard_map/all_to_all | solution.py:459
  49.1 25.5 %collective-permute-start = (bf16[16,16,2048]{2,1,0:T(8,128)(2,1)S(1)}, bf16[16,16,2048]{2,1,0:T(8,128)(2,1)S(1)}, u32[]{:S(2)}, u32[]{:S(2)}) collective-permute-start(bf16[16,16,2048]{2,1,0:T(8,128)(2,1)S(1)} %all-to-all-done.refs_0_), channel_id=1, source_target_pairs={{0,1},{1,0},{2,3},{3,2},{4,5},{5,4},{6,7},{7,6},{8,9},{9,8},{10,11... | collective-permute-start | bytes 3145736 | tf_op jit(solution)/shard_map/ppermute | solution.py:510
  74.6 1.0 copy-start.7
  74.6 1.3 copy-start.6
  75.9 46.9 %all-to-all-start.2 = ((bf16[16,32,2048]{2,1,0:T(8,128)(2,1)}), bf16[16,32,2048]{2,1,0:T(8,128)(2,1)S(1)}, u32[]{:S(2)}, u32[]{:S(2)}) async-start(bf16[16,32,2048]{2,1,0:T(8,128)(2,1)} %get-tuple-element.61), calls=%async_computation.2 | async-start | bytes 4194304 | tf_op jit(solution)/shard_map/all_to_all | solution.py:459
  81.7 25.8 %collective-permute-start.1 = (bf16[16,16,2048]{2,1,0:T(8,128)(2,1)}, bf16[16,16,2048]{2,1,0:T(8,128)(2,1)S(1)}, u32[]{:S(2)}, u32[]{:S(2)}) collective-permute-start(bf16[16,16,2048]{2,1,0:T(8,128)(2,1)} %copy-done.6), channel_id=1, source_target_pairs={{0,1},{1,0},{2,3},{3,2},{4,5},{5,4},{6,7},{7,6},{8,9},{9,8},{10,11... | collective-permute-start | bytes 3145736 | tf_op jit(solution)/shard_map/ppermute | solution.py:510
  107.5 1.0 copy-start.8
  122.8 34.3 %copy-start.1 = (bf16[16,32,2048]{2,1,0:T(8,128)(2,1)}, bf16[16,32,2048]{2,1,0:T(8,128)(2,1)S(1)}, u32[]{:S(2)}) copy-start(bf16[16,32,2048]{2,1,0:T(8,128)(2,1)S(1)} %all-to-all-done.2.refs_0_) | copy-start | bytes 6291460
  145.5 36.7 %all-to-all-start.3 = ((bf16[16,32,1152]{2,1,0:T(8,128)(2,1)}), bf16[16,32,1152]{2,1,0:T(8,128)(2,1)S(1)}, u32[]{:S(2)}, u32[]{:S(2)}) async-start(bf16[16,32,1152]{2,1,0:T(8,128)(2,1)} %bitcast.33), calls=%async_computation.3 | async-start | bytes 2359296 | tf_op jit(solution)/shard_map/all_to_all | solution.py:459
  157.1 48.1 %collective-permute-start.2 = (bf16[16,32,2048]{2,1,0:T(8,128)(2,1)S(1)}, bf16[16,32,2048]{2,1,0:T(8,128)(2,1)}, u32[]{:S(2)}, u32[]{:S(2)}) collective-permute-start(bf16[16,32,2048]{2,1,0:T(8,128)(2,1)S(1)} %all-to-all-done.2.refs_0_), channel_id=1, source_target_pairs={{0,1},{1,0},{2,3},{3,2},{4,5},{5,4},{6,7},{7,6},{8,9},{9,8},{10,11... | collective-permute-start | bytes 6291464 | tf_op jit(solution)/shard_map/ppermute | solution.py:510
  182.2 32.8 %copy-start.2 = (bf16[16,32,1152]{2,1,0:T(8,128)(2,1)}, bf16[16,32,1152]{2,1,0:T(8,128)(2,1)S(1)}, u32[]{:S(2)}) copy-start(bf16[16,32,1152]{2,1,0:T(8,128)(2,1)S(1)} %all-to-all-done.3.own_ref) | copy-start | bytes 3538948
  182.2 50.0 %all-to-all-start.4 = ((bf16[16,32,1152]{2,1,0:T(8,128)(2,1)}), bf16[16,32,1152]{2,1,0:T(8,128)(2,1)}, u32[]{:S(2)}, u32[]{:S(2)}) async-start(bf16[16,32,1152]{2,1,0:T(8,128)(2,1)} %bitcast.31), calls=%async_computation.4 | async-start | bytes 2359296 | tf_op jit(solution)/shard_map/all_to_all | solution.py:459
  232.2 31.2 %all-to-all-start.5 = ((bf16[16,32,1152]{2,1,0:T(8,128)(2,1)}), bf16[16,32,1152]{2,1,0:T(8,128)(2,1)S(1)}, u32[]{:S(2)}, u32[]{:S(2)}) async-start(bf16[16,32,1152]{2,1,0:T(8,128)(2,1)} %bitcast.34), calls=%async_computation.5 | async-start | bytes 2359296 | tf_op jit(solution)/shard_map/all_to_all | solution.py:459
  255.5 15.5 %copy-start.12 = (s32[16]{0:T(128)S(1)}, s32[16]{0:T(128)}, u32[]{:S(2)}) copy-start(s32[16]{0:T(128)} %order_ref.1) | copy-start | bytes 196
  263.4 8.2 %copy-start.3 = (bf16[16,32,1152]{2,1,0:T(8,128)(2,1)}, bf16[16,32,1152]{2,1,0:T(8,128)(2,1)S(1)}, u32[]{:S(2)}) copy-start(bf16[16,32,1152]{2,1,0:T(8,128)(2,1)S(1)} %all-to-all-done.5.guest_ref) | copy-start | bytes 3538948
  263.4 32.6 %all-to-all-start.6 = ((bf16[16,32,1152]{2,1,0:T(8,128)(2,1)}), bf16[16,32,1152]{2,1,0:T(8,128)(2,1)S(1)}, u32[]{:S(2)}, u32[]{:S(2)}) async-start(bf16[16,32,1152]{2,1,0:T(8,128)(2,1)} %bitcast.32), calls=%async_computation.6 | async-start | bytes 2359296 | tf_op jit(solution)/shard_map/all_to_all | solution.py:459
  270.9 82.7 %reduce-scatter.2.cloned.1.call-start = ((), (), s32[]{:S(2)}) async-start(), calls=%async_computation.8 | async-start | bytes 3145728 | tf_op jit(solution)/shard_map/reduce_scatter | solution.py:609
  296.0 1.0 copy-start.4
  305.4 46.5 %collective-permute-start.3 = (bf16[512,1024]{1,0:T(8,128)(2,1)}, bf16[512,1024]{1,0:T(8,128)(2,1)S(1)}, u32[]{:S(2)}, u32[]{:S(2)}) collective-permute-start(bf16[512,1024]{1,0:T(8,128)(2,1)} %get-tuple-element.98), channel_id=1, source_target_pairs={{0,1},{1,0},{2,3},{3,2},{4,5},{5,4},{6,7},{7,6},{8,9},{9,8},{10,11... | collective-permute-start | bytes 3145736 | tf_op jit(solution)/shard_map/ppermute | solution.py:606
Sparse Core Ops, SparseCore 0:
  296.2 55.3 reduce-scatter.1
where the time goes:
time: 365 us; the launch traced here: 363 us
  Pallas kernels  152 us (42%)
  waiting for transfers between devices  115 us (32%)
  starting transfers between devices  59.2 us (16%)
  between operations  16.1 us (4%)
  other arithmetic  14.8 us (4%)
  local copies, waits for them, and re-layouts  5.67 us (2%)
    pallas_call x4, Pallas kernels, attend(): pl.pallas_call(functools.partial(attend_kernel, causal, chunk, chunks, ro...  79.5 us
    all_to_all x7, starting transfers between devices, exchange(): return lax.all_to_all(value, 'grp', split_axis=0, concat_axis=0, tiled=True)  52.8 us
    ppermute x1, waiting for transfers between devices, summed(): arrived = lax.ppermute(theirs, 'tp', neighbour).astype(jnp.float32)  45 us
    ppermute x3, waiting for transfers between devices, with_other(): return [arrived, lax.ppermute(arrived, 'tp', neighbour)]  40.9 us
    pallas_call x4, Pallas kernels, project(): pl.pallas_call(functools.partial(project_kernel, turned, block // HEAD_DI...  40.1 us
    all_to_all x7, waiting for transfers between devices, exchange(): return lax.all_to_all(value, 'grp', split_axis=0, concat_axis=0, tiled=True)  29.5 us
    pallas_call x2, Pallas kernels, merge(): pl.pallas_call(functools.partial(merge_kernel, groups, heads), grid_spec=...  16.4 us
    pallas_call x1, Pallas kernels, replace_rows(): pl.pallas_call(functools.partial(replace_kernel, block), grid=(2, rows //...  10.9 us
  transfers between devices with their start and end apart: 12, of which 9 were waited for; matrix products, arithmetic and copies ran while one was open for 4% of the time, Pallas kernels for 34%

commit v1 on v0

--- a/solution.py
+++ b/solution.py
@@ -133,8 +133,8 @@
         out_shape=[jax.ShapeDtypeStruct((rows, width), jnp.bfloat16)] * count,
         compiler_params=params(),
         cost_estimate=pl.CostEstimate(
-            flops=rows * depth * width,
-            bytes_accessed=rows * depth,
+            flops=2 * rows * depth * width * count,
+            bytes_accessed=2 * (rows * depth + count * width * (rows + depth)),
             transcendentals=0,
         ),
         name="project",
@@ -322,13 +322,13 @@
             o_ref[rows, o_ref.shape[1] - STATS :] = packed.astype(jnp.bfloat16)
 
 
-def attend(count, rows_in, groups, chunk, chunks, sides, query, cache, new=()):
-    queries, q_at = query
+def attend(count, groups, chunk, chunks, sides, queries, cache, new=()):
     width = queries.shape[1]
     heads = width // HEAD_DIM
     per_step = 2
     rows = cache.shape[-2]
     causal = len(new) > 0
+    rows_in = queries.shape[0]
     lead = cache.ndim - 3
     shape = (1,) * (lead + 1) + (rows, per_step * HEAD_DIM)
     every = pl.BlockSpec((rows_in, per_step * HEAD_DIM), lambda h, n: (0, h))
@@ -343,7 +343,7 @@
             num_scalar_prefetch=1,
             grid=(heads // per_step,),
             in_specs=[
-                pl.BlockSpec((rows_in, per_step * HEAD_DIM), lambda h, n: (q_at, h)),
+                pl.BlockSpec((rows_in, per_step * HEAD_DIM), lambda h, n: (0, h)),
                 half(0),
                 half(1),
             ]
@@ -358,8 +358,8 @@
         out_shape=jax.ShapeDtypeStruct((rows_in, width + STATS), jnp.bfloat16),
         compiler_params=params(),
         cost_estimate=pl.CostEstimate(
-            flops=2 * rows_in * keys_seen * width,
-            bytes_accessed=4 * rows_in * width,
+            flops=16 * rows_in * keys_seen * width,
+            bytes_accessed=4 * rows * width + 4 * rows_in * width,
             transcendentals=0,
         ),
         name="attend_own" if causal else "attend_guest",
@@ -529,22 +529,12 @@
 
     def own_attend(chunk, queries):
         count = own_len[group_id][None]
-        rows_in = span // chunks
-        return attend(count, rows_in, groups, chunk, chunks, sides, (queries, 0), cache, new)
-
-    def guest_attend(chunk, query):
+        return attend(count, groups, chunk, chunks, sides, queries, cache, new)
+
+    def guest_attend(chunk, x):
+        (queries,) = projected(x, guest_tables, chunk, (w_query,), (True,))
         count = guest_len[group_id][None]
-        rows_in = span // chunks
-        return attend(count, rows_in, groups, chunk, chunks, sides, query, guest_cache)
-
-    def guest_project():
-        if paired:
-            (queries,) = projected(guest_x, guest_tables, 0, (w_query,), (True,))
-            return [(queries, 0), (queries, 1)]
-        return [
-            (projected(guest_x[chunk], guest_tables, chunk, (w_query,), (True,))[0], 0)
-            for chunk in range(chunks)
-        ]
+        return attend(count, groups, chunk, chunks, sides, queries, guest_cache)
 
     own_tables = rope_tables(place(group_id, partner_id))
     guest_tables = rope_tables(place(partner_id, group_id))
@@ -565,7 +555,9 @@
         arrived = exchange(guest_rows)
         made = [own_project(chunk) for chunk in range(chunks)]
         arrived, made = tied((arrived, made))
-        guest_x = with_other(arrived)
+        guest_x = [with_other(arrived[:, :each])]
+        guest_x, arrived = tied((guest_x, arrived[:, each:]))
+        guest_x.append(with_other(arrived))
     else:
         cache = replace_rows(own_cache, *rec_parts, rec_index)
         own_x = gathered(own_rows)
@@ -581,27 +573,26 @@
         axis=1,
     )
 
-    own_out = [own_attend(0, made[0][0])]
-    own_out, query = tied((own_out, made[1][0]))
-    own_part = [exchange(own_out[0])]
-    own_out.append(own_attend(1, query))
-    own_part, own_out = tied((own_part, own_out))
-    own_part.append(exchange(own_out[1]))
-    guest_x, own_out = tied((guest_x, own_out))
-    queries = guest_project()
-    guest_out = [guest_attend(0, queries[0])]
-    own_part, guest_out, query = tied((own_part, guest_out, queries[1][0]))
-    guest_part = [exchange(guest_out[0])]
-    guest_out.append(guest_attend(1, (query, queries[1][1])))
-    guest_part, guest_out = tied((guest_part, guest_out))
-    guest_part.append(exchange(guest_out[1]))
+    first, second = guest_x
+    own_out = own_attend(0, made[0][0])
+    own_out, query, first = tied((own_out, made[1][0], first))
+    own_part = [exchange(own_out)]
+    guest_out = guest_attend(0, first)
+    own_part, guest_out, query = tied((own_part, guest_out, query))
+    guest_part = [exchange(guest_out)]
+    own_out = own_attend(1, query)
+    guest_part, own_out, second = tied((guest_part, own_out, second))
+    own_part.append(exchange(own_out))
+    guest_out = guest_attend(1, second)
+    own_part, guest_out = tied((own_part, guest_out))
+    guest_part.append(exchange(guest_out))
 
     def merged(chunk):
-        splits = 2 if paired and chunk else 1
+        splits = 2 if paired else 1
         return merge(inverse, tp_index, splits, own_part[chunk], guest_part[chunk], w_out)
 
-    def summed(partial, split):
-        if split:
+    def summed(partial):
+        if paired:
             theirs, mine = partial
             arrived = lax.ppermute(theirs, "tp", neighbour).astype(jnp.float32)
             total = (mine.astype(jnp.float32) + arrived).astype(jnp.bfloat16)
@@ -609,9 +600,9 @@
             total = lax.psum_scatter(partial[0], "tp", scatter_dimension=1, tiled=True)
         return total.reshape(groups, sides, 1, each, -1)
 
-    partial = merged(0)
-    guest_part[1], partial = tied((guest_part[1], partial))
-    mixed = [summed(partial, False), summed(merged(1), paired)]
+    mixed = [summed(merged(0))]
+    guest_part[1], mixed = tied((guest_part[1], mixed))
+    mixed.append(summed(merged(1)))
     return jnp.concatenate(mixed, axis=2).reshape(groups, shard_rows, -1)
 
 

time: 365 us -> 327 us (0.90)
  waiting for transfers between devices: 115 us -> 83 us
  between operations: 16.1 us -> 2.8 us
  Pallas kernels: 152 us -> 156 us
    all_to_all x7, waiting for transfers between devices: 29.5 us -> 6.47 us  [exchange(): return lax.all_to_all(value, 'grp', split_axis=0, concat_axis=0, tiled=True)]
    ppermute x3 -> x4, waiting for transfers between devices: 40.9 us -> 29 us  [with_other(): return [arrived, lax.ppermute(arrived, 'tp', neighbour)]]
    pallas_call x4 -> x5, Pallas kernels: 40.1 us -> 43.7 us  [project(): pl.pallas_call(functools.partial(project_kernel, turned, block // HEAD_DI...]
    ppermute x1 -> x2, waiting for transfers between devices: 45 us -> 47.6 us  [summed(): arrived = lax.ppermute(theirs, 'tp', neighbour).astype(jnp.float32)]
  transfers between devices with their start and end apart: 12 -> 13, of which waited for: 9 -> 10; matrix products, arithmetic and copies ran while one was open for 4% -> 4% of each run, Pallas kernels for 34% -> 44%
where the time goes in v1:
time: 327 us; the launch traced here: 326 us
  Pallas kernels  156 us (48%)
  waiting for transfers between devices  83 us (25%)
  starting transfers between devices  62.1 us (19%)
  other arithmetic  15.2 us (5%)
  local copies, waits for them, and re-layouts  6.94 us (2%)
    pallas_call x4, Pallas kernels, attend(): pl.pallas_call(functools.partial(attend_kernel, causal, chunk, chunks, ro...  79.5 us
    all_to_all x7, starting transfers between devices, exchange(): return lax.all_to_all(value, 'grp', split_axis=0, concat_axis=0, tiled=True)  52.8 us
    ppermute x2, waiting for transfers between devices, summed(): arrived = lax.ppermute(theirs, 'tp', neighbour).astype(jnp.float32)  47.6 us
    pallas_call x5, Pallas kernels, project(): pl.pallas_call(functools.partial(project_kernel, turned, block // HEAD_DI...  43.7 us
    ppermute x4, waiting for transfers between devices, with_other(): return [arrived, lax.ppermute(arrived, 'tp', neighbour)]  29 us
    pallas_call x2, Pallas kernels, merge(): pl.pallas_call(functools.partial(merge_kernel, groups, heads), grid_spec=...  16.5 us
    pallas_call x1, Pallas kernels, replace_rows(): pl.pallas_call(functools.partial(replace_kernel, block), grid=(2, rows //...  10.9 us
  transfers between devices with their start and end apart: 13, of which 10 were waited for; matrix products, arithmetic and copies ran while one was open for 4% of the time, Pallas kernels for 44%

profile of v1, /device:TPU:0, one launch (start us, length us, event | category | flops | bytes accessed | tf_op | source)
XLA Modules:
  0.0 325.9 jit_solution(15831359839258736738)
XLA Ops:
  0.0 5.3 %deal.1 = (bf16[16,16,2048]{2,1,0:T(8,128)(2,1)}, bf16[16,16,2048]{2,1,0:T(8,128)(2,1)}, bf16[16,32,2048]{2,1,0:T(8,128)(2,1)}) custom-call(s32[16]{0:T(128)} %order_ref.1, s32[1]{0:T(128)} %bitcast.tp_ref, bf16[16,64,2048]{2,1,0:T(8,128)(2,1)} %x_ref.1), custom_call_target="tpu_custom_call" | custom-call | tf_op jit(solution)/shard_map/deal/pallas_call | solution.py:64
  5.3 7.5 %all-to-all-start = ((bf16[16,16,2048]{2,1,0:T(8,128)(2,1)}), bf16[16,16,2048]{2,1,0:T(8,128)(2,1)S(1)}, u32[]{:S(2)}, u32[]{:S(2)}) async-start(bf16[16,16,2048]{2,1,0:T(8,128)(2,1)} %get-tuple-element.59), calls=%async_computation | async-start | bytes 2097152 | tf_op jit(solution)/shard_map/all_to_all | solution.py:459
  16.3 3.7 %fusion.6 = (f32[1024,64]{1,0:T(8,128)S(1)}, f32[1024,64]{1,0:T(8,128)S(1)}, f32[1024,64]{1,0:T(8,128)S(1)}, f32[1024,64]{1,0:T(8,128)S(1)}, f32[1024,64]{1,0:T(8,128)S(1)}, /*index=5*/f32[1024,64]{1,0:T(8,128)S(1)}) fusion(f32[64]{0:T(128)S(1)} %multiply_exponential_fusion, f32[1024]{0:T(1024)S(1)} %convert_element_type.68, f32[1024]{0:T(1024)S(1)} %convert_element_type.65), kind=kLoop, calls=%fused_computation.21 | loop fusion | flops 262144 | bytes 1581312 | tf_op jit(solution)/shard_map/neg | solution.py:43
  27.4 6.8 %project.5 = (bf16[256,1024]{1,0:T(8,128)(2,1)}, bf16[256,1024]{1,0:T(8,128)(2,1)}) custom-call(s32[1]{0:T(128)} %bitcast.tp_ref, bf16[256,2048]{1,0:T(8,128)(2,1)} %fusion.4.refs_0_, f32[256,128]{1,0:T(8,128)} %get-tuple-element.133.refs_1_, f32[256,128]{1,0:T(8,128)} %get-tuple-element.134.refs_2_, bf16[2048,1024]{1,0:T(8,128)(2,1)} %refs_5_.3, ...), custom_call_target="tpu_custom_call" | custom-call | flops 2147483648 | bytes 10485760 | tf_op jit(solution)/shard_map/project/pallas_call | solution.py:122
  35.7 6.9 %all-to-all-start.1 = ((bf16[16,16,2048]{2,1,0:T(8,128)(2,1)}), bf16[16,16,2048]{2,1,0:T(8,128)(2,1)S(1)}, u32[]{:S(2)}, u32[]{:S(2)}) async-start(bf16[16,16,2048]{2,1,0:T(8,128)(2,1)} %get-tuple-element.63), calls=%async_computation.1 | async-start | bytes 2097152 | tf_op jit(solution)/shard_map/all_to_all | solution.py:459
  42.6 1.6 collective-permute-start
  44.2 10.9 %replace_rows.1.k_ref.v_ref = bf16[2,2048,1024]{2,1,0:T(8,128)(2,1)} custom-call(s32[1,256]{1,0:T(1,128)} %index_ref.1, bf16[1,2,2048,1024]{3,2,1,0:T(8,128)(2,1)} %cache_ref.1, bf16[256,1024]{1,0:T(8,128)(2,1)} %get-tuple-element.64.keys_ref, bf16[256,1024]{1,0:T(8,128)(2,1)} %get-tuple-element.65.values_ref), custom_call_target="tpu_custom_call" | custom-call | flops 2147483648 | bytes 20971520 | tf_op jit(solution)/shard_map/replace_rows/pallas_call | solution.py:167
  55.1 13.0 %collective-permute-done.refs_1_ = bf16[16,16,2048]{2,1,0:T(8,128)(2,1)S(1)} collective-permute-done((bf16[16,16,2048]{2,1,0:T(8,128)(2,1)S(1)}, bf16[16,16,2048]{2,1,0:T(8,128)(2,1)S(1)}, u32[]{:S(2)}, u32[]{:S(2)}) %collective-permute-start) | collective-permute-done | bytes 1048608 | tf_op jit(solution)/shard_map/ppermute | solution.py:510
  69.4 5.8 %all-to-all-start.2 = ((bf16[16,32,2048]{2,1,0:T(8,128)(2,1)}), bf16[16,32,2048]{2,1,0:T(8,128)(2,1)S(1)}, u32[]{:S(2)}, u32[]{:S(2)}) async-start(bf16[16,32,2048]{2,1,0:T(8,128)(2,1)} %get-tuple-element.68), calls=%async_computation.2 | async-start | bytes 4194304 | tf_op jit(solution)/shard_map/all_to_all | solution.py:459
  75.2 1.6 collective-permute-start.1
  76.8 11.8 %project.6 = (bf16[512,1024]{1,0:T(8,128)(2,1)}, bf16[512,1024]{1,0:T(8,128)(2,1)}, bf16[512,1024]{1,0:T(8,128)(2,1)}) custom-call(s32[1]{0:T(128)} %bitcast.tp_ref, bf16[16,16,2048]{2,1,0:T(8,128)(2,1)} %copy-done.7, bf16[16,16,2048]{2,1,0:T(8,128)(2,1)} %copy-done.13, f32[1024,128]{1,0:T(8,128)} %pad_maximum_fusion.1.refs_2_, ...), custom_call_target="tpu_custom_call" | custom-call | flops 6442450944 | bytes 17825792 | tf_op jit(solution)/shard_map/project/pallas_call | solution.py:122
  88.5 12.4 %collective-permute-done.1.refs_1_ = bf16[16,16,2048]{2,1,0:T(8,128)(2,1)S(1)} collective-permute-done((bf16[16,16,2048]{2,1,0:T(8,128)(2,1)}, bf16[16,16,2048]{2,1,0:T(8,128)(2,1)S(1)}, u32[]{:S(2)}, u32[]{:S(2)}) %collective-permute-start.1) | collective-permute-done | bytes 1048608 | tf_op jit(solution)/shard_map/ppermute | solution.py:510
  101.9 11.7 %project.7 = (bf16[512,1024]{1,0:T(8,128)(2,1)}, bf16[512,1024]{1,0:T(8,128)(2,1)}, bf16[512,1024]{1,0:T(8,128)(2,1)}) custom-call(s32[1]{0:T(128)} %bitcast.tp_ref, bf16[16,16,2048]{2,1,0:T(8,128)(2,1)} %copy-done.8, bf16[16,16,2048]{2,1,0:T(8,128)(2,1)} %copy-done.14, f32[1024,128]{1,0:T(8,128)} %pad_maximum_fusion.1.refs_2_, ...), custom_call_target="tpu_custom_call" | custom-call | flops 6442450944 | bytes 17825792 | tf_op jit(solution)/shard_map/project/pallas_call | solution.py:122
  113.7 2.6 all-to-all-done.2
  119.0 22.5 %attend_own.2 = bf16[512,1152]{1,0:T(8,128)(2,1)} custom-call(s32[1]{0:T(128)} %get-tuple-element.131.count_ref, bf16[512,1024]{1,0:T(8,128)(2,1)} %get-tuple-element.80.q_ref, bf16[2,2048,1024]{2,1,0:T(8,128)(2,1)} %replace_rows.1.k_ref.v_ref, bf16[2,2048,1024]{2,1,0:T(8,128)(2,1)} %replace_rows.1.k_ref.v_ref, bf16[512,1024]{1,0:T(8,128)(2,1)} %get-tuple-element.82.refs_0_, ...), custom_call_target="tpu_custom_call" | custom-call | flops 21474836480 | bytes 10485760 | tf_op jit(solution)/shard_map/attend_own/pallas_call | solution.py:340
  141.5 2.0 collective-permute-done.2.refs_1_
  143.5 10.8 %all-to-all-start.3 = ((bf16[16,32,1152]{2,1,0:T(8,128)(2,1)}), bf16[16,32,1152]{2,1,0:T(8,128)(2,1)S(1)}, u32[]{:S(2)}, u32[]{:S(2)}) async-start(bf16[16,32,1152]{2,1,0:T(8,128)(2,1)} %bitcast.36), calls=%async_computation.3 | async-start | bytes 2359296 | tf_op jit(solution)/shard_map/all_to_all | solution.py:459
  154.3 6.7 %project.8.q_ref = bf16[512,1024]{1,0:T(8,128)(2,1)} custom-call(s32[1]{0:T(128)} %bitcast.tp_ref, bf16[16,16,2048]{2,1,0:T(8,128)(2,1)} %get-tuple-element.91.refs_0_, bf16[16,16,2048]{2,1,0:T(8,128)(2,1)} %copy-done.6, f32[1024,128]{1,0:T(8,128)} %pad_maximum_fusion.3.refs_2_, f32[1024,128]{1,0:T(8,128)} %pad_maximum_fusion.4.refs_3_, ...), custom_call_target="tpu_custom_call" | custom-call | flops 2147483648 | bytes 7340032 | tf_op jit(solution)/shard_map/project/pallas_call | solution.py:122
  161.0 17.2 %attend_guest.2 = bf16[512,1152]{1,0:T(8,128)(2,1)} custom-call(s32[1]{0:T(128)} %get-tuple-element.127.count_ref, bf16[512,1024]{1,0:T(8,128)(2,1)} %project.8.q_ref, bf16[1,2,2048,1024]{3,2,1,0:T(8,128)(2,1)} %v_ref.3, bf16[1,2,2048,1024]{3,2,1,0:T(8,128)(2,1)} %v_ref.3), custom_call_target="tpu_custom_call" | custom-call | flops 17179869184 | bytes 10485760 | tf_op jit(solution)/shard_map/attend_guest/pallas_call | solution.py:340
  179.4 7.5 %all-to-all-start.4 = ((bf16[16,32,1152]{2,1,0:T(8,128)(2,1)}), bf16[16,32,1152]{2,1,0:T(8,128)(2,1)S(1)}, u32[]{:S(2)}, u32[]{:S(2)}) async-start(bf16[16,32,1152]{2,1,0:T(8,128)(2,1)} %bitcast.35), calls=%async_computation.4 | async-start | bytes 2359296 | tf_op jit(solution)/shard_map/all_to_all | solution.py:459
  186.9 1.6 collective-permute-start.3
  188.5 22.5 %attend_own.3 = bf16[512,1152]{1,0:T(8,128)(2,1)} custom-call(s32[1]{0:T(128)} %get-tuple-element.131.count_ref, bf16[512,1024]{1,0:T(8,128)(2,1)} %get-tuple-element.98.q_ref, bf16[2,2048,1024]{2,1,0:T(8,128)(2,1)} %replace_rows.1.k_ref.v_ref, bf16[2,2048,1024]{2,1,0:T(8,128)(2,1)} %replace_rows.1.k_ref.v_ref, bf16[512,1024]{1,0:T(8,128)(2,1)} %get-tuple-element.82.refs_0_, ...), custom_call_target="tpu_custom_call" | custom-call | flops 21474836480 | bytes 10485760 | tf_op jit(solution)/shard_map/attend_own/pallas_call | solution.py:340
  212.6 6.9 %all-to-all-start.5 = ((bf16[16,32,1152]{2,1,0:T(8,128)(2,1)}), bf16[16,32,1152]{2,1,0:T(8,128)(2,1)S(1)}, u32[]{:S(2)}, u32[]{:S(2)}) async-start(bf16[16,32,1152]{2,1,0:T(8,128)(2,1)} %bitcast.34), calls=%async_computation.5 | async-start | bytes 2359296 | tf_op jit(solution)/shard_map/all_to_all | solution.py:459
  219.5 6.7 %project.9.q_ref = bf16[512,1024]{1,0:T(8,128)(2,1)} custom-call(s32[1]{0:T(128)} %bitcast.tp_ref, bf16[16,16,2048]{2,1,0:T(8,128)(2,1)} %copy-done.5, bf16[16,16,2048]{2,1,0:T(8,128)(2,1)} %collective-permute-done.3.refs_1_, f32[1024,128]{1,0:T(8,128)} %pad_maximum_fusion.3.refs_2_, f32[1024,128]{1,0:T(8,128)} %pad_maximum_fusion.4.refs_3_, ...), custom_call_target="tpu_custom_call" | custom-call | flops 2147483648 | bytes 7340032 | tf_op jit(solution)/shard_map/project/pallas_call | solution.py:122
  226.2 17.2 %attend_guest.3 = bf16[512,1152]{1,0:T(8,128)(2,1)} custom-call(s32[1]{0:T(128)} %get-tuple-element.127.count_ref, bf16[512,1024]{1,0:T(8,128)(2,1)} %project.9.q_ref, bf16[1,2,2048,1024]{3,2,1,0:T(8,128)(2,1)} %v_ref.3, bf16[1,2,2048,1024]{3,2,1,0:T(8,128)(2,1)} %v_ref.3), custom_call_target="tpu_custom_call" | custom-call | flops 17179869184 | bytes 10485760 | tf_op jit(solution)/shard_map/attend_guest/pallas_call | solution.py:340
  244.6 7.5 %all-to-all-start.6 = ((bf16[16,32,1152]{2,1,0:T(8,128)(2,1)}), bf16[16,32,1152]{2,1,0:T(8,128)(2,1)S(1)}, u32[]{:S(2)}, u32[]{:S(2)}) async-start(bf16[16,32,1152]{2,1,0:T(8,128)(2,1)} %bitcast.33), calls=%async_computation.6 | async-start | bytes 2359296 | tf_op jit(solution)/shard_map/all_to_all | solution.py:459
  252.8 8.2 %merge.2 = (bf16[512,1024]{1,0:T(8,128)(2,1)}, bf16[512,1024]{1,0:T(8,128)(2,1)}) custom-call(s32[16]{0:T(128)} %select_reduce_fusion.inverse_ref, s32[1]{0:T(128)} %bitcast.tp_ref, bf16[16,32,1152]{2,1,0:T(8,128)(2,1)} %copy-done.1, bf16[16,32,1152]{2,1,0:T(8,128)(2,1)} %copy-done.2, bf16[1024,2048]{1,0:T(8,128)(2,1)} %w_ref.3), custom_call_target="tpu_custom_call" | custom-call | flops 1073741824 | bytes 1048576 | tf_op jit(solution)/shard_map/merge/pallas_call | solution.py:435
  262.5 24.2 %collective-permute-done.4 = bf16[512,1024]{1,0:T(8,128)(2,1)S(1)} collective-permute-done((bf16[512,1024]{1,0:T(8,128)(2,1)}, bf16[512,1024]{1,0:T(8,128)(2,1)S(1)}, u32[]{:S(2)}, u32[]{:S(2)}) %collective-permute-start.4) | collective-permute-done | bytes 1048608 | tf_op jit(solution)/shard_map/ppermute | solution.py:597
  286.7 1.6 add_convert_fusion.1
  289.4 8.3 %merge.3 = (bf16[512,1024]{1,0:T(8,128)(2,1)}, bf16[512,1024]{1,0:T(8,128)(2,1)}) custom-call(s32[16]{0:T(128)} %select_reduce_fusion.inverse_ref, s32[1]{0:T(128)} %bitcast.tp_ref, bf16[16,32,1152]{2,1,0:T(8,128)(2,1)} %copy-done.3, bf16[16,32,1152]{2,1,0:T(8,128)(2,1)} %copy-done.4, bf16[1024,2048]{1,0:T(8,128)(2,1)} %w_ref.3), custom_call_target="tpu_custom_call" | custom-call | flops 1073741824 | bytes 1048576 | tf_op jit(solution)/shard_map/merge/pallas_call | solution.py:435
  299.2 23.4 %collective-permute-done.5 = bf16[512,1024]{1,0:T(8,128)(2,1)S(1)} collective-permute-done((bf16[512,1024]{1,0:T(8,128)(2,1)}, bf16[512,1024]{1,0:T(8,128)(2,1)S(1)}, u32[]{:S(2)}, u32[]{:S(2)}) %collective-permute-start.5) | collective-permute-done | bytes 1048608 | tf_op jit(solution)/shard_map/ppermute | solution.py:597
  322.6 1.6 add_convert_fusion
  (62 shorter events, 25.2 us)
Async XLA Ops:
  5.3 7.5 %copy-start.10 = (s32[16]{0:T(128)S(1)}, s32[16]{0:T(128)}, u32[]{:S(2)}) copy-start(s32[16]{0:T(128)} %param.22) | copy-start | bytes 196
  5.3 7.5 %copy-start.11 = (s32[16]{0:T(128)S(1)}, s32[16]{0:T(128)}, u32[]{:S(2)}) copy-start(s32[16]{0:T(128)} %param.21) | copy-start | bytes 196
  5.3 30.4 %all-to-all-start = ((bf16[16,16,2048]{2,1,0:T(8,128)(2,1)}), bf16[16,16,2048]{2,1,0:T(8,128)(2,1)S(1)}, u32[]{:S(2)}, u32[]{:S(2)}) async-start(bf16[16,16,2048]{2,1,0:T(8,128)(2,1)} %get-tuple-element.59), calls=%async_computation | async-start | bytes 2097152 | tf_op jit(solution)/shard_map/all_to_all | solution.py:459
  16.3 4.7 %copy-start.9 = (s32[1,256]{1,0:T(1,128)S(1)}, s32[1,256]{1,0:T(1,128)}, u32[]{:S(2)}) copy-start(s32[1,256]{1,0:T(1,128)} %index_ref.1) | copy-start | bytes 3076
  22.5 3.0 copy-start
  35.7 19.4 %copy-start.7 = (bf16[16,16,2048]{2,1,0:T(8,128)(2,1)}, bf16[16,16,2048]{2,1,0:T(8,128)(2,1)S(1)}, u32[]{:S(2)}) copy-start(bf16[16,16,2048]{2,1,0:T(8,128)(2,1)S(1)} %all-to-all-done.refs_0_) | copy-start | bytes 3145732
  35.7 32.4 %all-to-all-start.1 = ((bf16[16,16,2048]{2,1,0:T(8,128)(2,1)}), bf16[16,16,2048]{2,1,0:T(8,128)(2,1)S(1)}, u32[]{:S(2)}, u32[]{:S(2)}) async-start(bf16[16,16,2048]{2,1,0:T(8,128)(2,1)} %get-tuple-element.63), calls=%async_computation.1 | async-start | bytes 2097152 | tf_op jit(solution)/shard_map/all_to_all | solution.py:459
  42.6 25.5 %collective-permute-start = (bf16[16,16,2048]{2,1,0:T(8,128)(2,1)S(1)}, bf16[16,16,2048]{2,1,0:T(8,128)(2,1)S(1)}, u32[]{:S(2)}, u32[]{:S(2)}) collective-permute-start(bf16[16,16,2048]{2,1,0:T(8,128)(2,1)S(1)} %all-to-all-done.refs_0_), channel_id=1, source_target_pairs={{0,1},{1,0},{2,3},{3,2},{4,5},{5,4},{6,7},{7,6},{8,9},{9,8},{10,11... | collective-permute-start | bytes 3145736 | tf_op jit(solution)/shard_map/ppermute | solution.py:510
  68.1 1.0 copy-start.13
  68.1 1.3 copy-start.8
  69.4 46.9 %all-to-all-start.2 = ((bf16[16,32,2048]{2,1,0:T(8,128)(2,1)}), bf16[16,32,2048]{2,1,0:T(8,128)(2,1)S(1)}, u32[]{:S(2)}, u32[]{:S(2)}) async-start(bf16[16,32,2048]{2,1,0:T(8,128)(2,1)} %get-tuple-element.68), calls=%async_computation.2 | async-start | bytes 4194304 | tf_op jit(solution)/shard_map/all_to_all | solution.py:459
  75.2 25.8 %collective-permute-start.1 = (bf16[16,16,2048]{2,1,0:T(8,128)(2,1)}, bf16[16,16,2048]{2,1,0:T(8,128)(2,1)S(1)}, u32[]{:S(2)}, u32[]{:S(2)}) collective-permute-start(bf16[16,16,2048]{2,1,0:T(8,128)(2,1)} %copy-done.8), channel_id=1, source_target_pairs={{0,1},{1,0},{2,3},{3,2},{4,5},{5,4},{6,7},{7,6},{8,9},{9,8},{10,11... | collective-permute-start | bytes 3145736 | tf_op jit(solution)/shard_map/ppermute | solution.py:510
  100.9 1.0 copy-start.14
  117.4 69.4 %copy-start.5 = (bf16[16,16,2048]{2,1,0:T(8,128)(2,1)}, bf16[16,16,2048]{2,1,0:T(8,128)(2,1)S(1)}, u32[]{:S(2)}) copy-start(bf16[16,16,2048]{2,1,0:T(8,128)(2,1)S(1)} %get-tuple-element.101.refs_0_) | copy-start | bytes 3145732
  117.4 26.0 %collective-permute-start.2 = (bf16[16,16,2048]{2,1,0:T(8,128)(2,1)}, bf16[16,16,2048]{2,1,0:T(8,128)(2,1)S(1)}, u32[]{:S(2)}, u32[]{:S(2)}) collective-permute-start(bf16[16,16,2048]{2,1,0:T(8,128)(2,1)} %get-tuple-element.91.refs_0_), channel_id=1, source_target_pairs={{0,1},{1,0},{2,3},{3,2},{4,5},{5,4},{6,7},{7,6},{8,9},{9,8},{10,11... | collective-permute-start | bytes 3145736 | tf_op jit(solution)/shard_map/ppermute | solution.py:510
  143.5 10.8 %copy-start.6 = (bf16[16,16,2048]{2,1,0:T(8,128)(2,1)}, bf16[16,16,2048]{2,1,0:T(8,128)(2,1)S(1)}, u32[]{:S(2)}) copy-start(bf16[16,16,2048]{2,1,0:T(8,128)(2,1)S(1)} %collective-permute-done.2.refs_1_) | copy-start | bytes 3145732
  143.5 35.9 %all-to-all-start.3 = ((bf16[16,32,1152]{2,1,0:T(8,128)(2,1)}), bf16[16,32,1152]{2,1,0:T(8,128)(2,1)S(1)}, u32[]{:S(2)}, u32[]{:S(2)}) async-start(bf16[16,32,1152]{2,1,0:T(8,128)(2,1)} %bitcast.36), calls=%async_computation.3 | async-start | bytes 2359296 | tf_op jit(solution)/shard_map/all_to_all | solution.py:459
  179.4 31.6 %copy-start.1 = (bf16[16,32,1152]{2,1,0:T(8,128)(2,1)}, bf16[16,32,1152]{2,1,0:T(8,128)(2,1)S(1)}, u32[]{:S(2)}) copy-start(bf16[16,32,1152]{2,1,0:T(8,128)(2,1)S(1)} %all-to-all-done.3.own_ref) | copy-start | bytes 3538948
  179.4 33.2 %all-to-all-start.4 = ((bf16[16,32,1152]{2,1,0:T(8,128)(2,1)}), bf16[16,32,1152]{2,1,0:T(8,128)(2,1)S(1)}, u32[]{:S(2)}, u32[]{:S(2)}) async-start(bf16[16,32,1152]{2,1,0:T(8,128)(2,1)} %bitcast.35), calls=%async_computation.4 | async-start | bytes 2359296 | tf_op jit(solution)/shard_map/all_to_all | solution.py:459
  186.9 25.7 %collective-permute-start.3 = (bf16[16,16,2048]{2,1,0:T(8,128)(2,1)S(1)}, bf16[16,16,2048]{2,1,0:T(8,128)(2,1)}, u32[]{:S(2)}, u32[]{:S(2)}) collective-permute-start(bf16[16,16,2048]{2,1,0:T(8,128)(2,1)S(1)} %get-tuple-element.101.refs_0_), channel_id=1, source_target_pairs={{0,1},{1,0},{2,3},{3,2},{4,5},{5,4},{6,7},{7,6},{8,9},{9,8},{10,11... | collective-permute-start | bytes 3145736 | tf_op jit(solution)/shard_map/ppermute | solution.py:510
  212.5 13.7 %copy-start.2 = (bf16[16,32,1152]{2,1,0:T(8,128)(2,1)}, bf16[16,32,1152]{2,1,0:T(8,128)(2,1)S(1)}, u32[]{:S(2)}) copy-start(bf16[16,32,1152]{2,1,0:T(8,128)(2,1)S(1)} %all-to-all-done.4.guest_ref) | copy-start | bytes 3538948
  212.6 32.1 %all-to-all-start.5 = ((bf16[16,32,1152]{2,1,0:T(8,128)(2,1)}), bf16[16,32,1152]{2,1,0:T(8,128)(2,1)S(1)}, u32[]{:S(2)}, u32[]{:S(2)}) async-start(bf16[16,32,1152]{2,1,0:T(8,128)(2,1)} %bitcast.34), calls=%async_computation.5 | async-start | bytes 2359296 | tf_op jit(solution)/shard_map/all_to_all | solution.py:459
  243.4 8.7 %copy-start.12 = (s32[16]{0:T(128)S(1)}, s32[16]{0:T(128)}, u32[]{:S(2)}) copy-start(s32[16]{0:T(128)} %order_ref.1) | copy-start | bytes 196
  244.6 16.4 %copy-start.3 = (bf16[16,32,1152]{2,1,0:T(8,128)(2,1)}, bf16[16,32,1152]{2,1,0:T(8,128)(2,1)S(1)}, u32[]{:S(2)}) copy-start(bf16[16,32,1152]{2,1,0:T(8,128)(2,1)S(1)} %all-to-all-done.5.own_ref) | copy-start | bytes 3538948
  244.6 43.7 %all-to-all-start.6 = ((bf16[16,32,1152]{2,1,0:T(8,128)(2,1)}), bf16[16,32,1152]{2,1,0:T(8,128)(2,1)S(1)}, u32[]{:S(2)}, u32[]{:S(2)}) async-start(bf16[16,32,1152]{2,1,0:T(8,128)(2,1)} %bitcast.33), calls=%async_computation.6 | async-start | bytes 2359296 | tf_op jit(solution)/shard_map/all_to_all | solution.py:459
  261.0 25.7 %collective-permute-start.4 = (bf16[512,1024]{1,0:T(8,128)(2,1)}, bf16[512,1024]{1,0:T(8,128)(2,1)S(1)}, u32[]{:S(2)}, u32[]{:S(2)}) collective-permute-start(bf16[512,1024]{1,0:T(8,128)(2,1)} %get-tuple-element.107), channel_id=1, source_target_pairs={{0,1},{1,0},{2,3},{3,2},{4,5},{5,4},{6,7},{7,6},{8,9},{9,8},{10,11... | collective-permute-start | bytes 3145736 | tf_op jit(solution)/shard_map/ppermute | solution.py:597
  288.4 1.0 copy-start.4
  297.7 24.9 %collective-permute-start.5 = (bf16[512,1024]{1,0:T(8,128)(2,1)}, bf16[512,1024]{1,0:T(8,128)(2,1)S(1)}, u32[]{:S(2)}, u32[]{:S(2)}) collective-permute-start(bf16[512,1024]{1,0:T(8,128)(2,1)} %get-tuple-element.112), channel_id=1, source_target_pairs={{0,1},{1,0},{2,3},{3,2},{4,5},{5,4},{6,7},{7,6},{8,9},{9,8},{10,11... | collective-permute-start | bytes 3145736 | tf_op jit(solution)/shard_map/ppermute | solution.py:597

commit v2 on v1

--- a/solution.py
+++ b/solution.py
@@ -12,7 +12,6 @@
 KEY_BLOCK = 1024
 ROW_BLOCK = 256
 STATS = 128
-PIECE = 256
 VMEM_LIMIT = 60 * 1024 * 1024
 
 rope_base = 10000.0
@@ -188,38 +187,29 @@
 
     def scores_of(job):
         _, queries, keys, _ = job
+        parts = []
         for key_block, mask in keys():
-            for at in range(0, key_block.shape[0], PIECE):
-                scores = lax.dot_general(
-                    queries(),
-                    key_block[at : at + PIECE],
-                    (((1,), (1,)), ((), ())),
-                    preferred_element_type=jnp.float32,
-                )
-                if mask is not None:
-                    scores = jnp.where(mask[:, at : at + PIECE], scores, LOWEST)
-                yield scores
-
-    upcoming = list(scores_of(jobs[0]))
+            scores = lax.dot_general(
+                queries(), key_block, (((1,), (1,)), ((), ())), preferred_element_type=jnp.float32
+            )
+            parts.append(scores if mask is None else jnp.where(mask, scores, LOWEST))
+        return parts[0] if len(parts) == 1 else jnp.concatenate(parts, axis=1)
+
+    upcoming = scores_of(jobs[0])
     for at, (place, _, _, values) in enumerate(jobs):
         scores = upcoming
-        ahead = scores_of(jobs[at + 1]) if at + 1 < len(jobs) else iter(())
-        upcoming = []
+        if at + 1 < len(jobs):
+            upcoming = scores_of(jobs[at + 1])
         old_max = m_ref[place]
-        widest = functools.reduce(jnp.maximum, scores)
-        new_max = jnp.maximum(old_max, jnp.max(widest, axis=1, keepdims=True))
+        new_max = jnp.maximum(old_max, jnp.max(scores, axis=1, keepdims=True))
         factor = jnp.exp2((old_max - new_max) * scale)
         shift = new_max * scale
-        shift = jnp.concatenate([shift] * (PIECE // HEAD_DIM), axis=1)
-        weights = []
-        for part in scores:
-            upcoming += [found for _, found in zip(range(1), ahead)]
-            weights.append(jnp.exp2(part * scale - shift).astype(jnp.bfloat16))
-        upcoming += list(ahead)
+        tiles = scores.shape[1] // HEAD_DIM
+        weights = jnp.exp2(scores * scale - jnp.concatenate([shift] * tiles, axis=1))
         seen = values()
         widened = jnp.concatenate([seen, jnp.ones(seen.shape, jnp.bfloat16)], axis=1)
         product = jnp.dot(
-            jnp.concatenate(weights, axis=1), widened, preferred_element_type=jnp.float32
+            weights.astype(jnp.bfloat16), widened, preferred_element_type=jnp.float32
         )
         acc_ref[place] = acc_ref[place] * jnp.concatenate([factor, factor], axis=1) + product
         m_ref[place] = new_max
@@ -584,8 +574,6 @@
     guest_part, own_out, second = tied((guest_part, own_out, second))
     own_part.append(exchange(own_out))
     guest_out = guest_attend(1, second)
-    own_part, guest_out = tied((own_part, guest_out))
-    guest_part.append(exchange(guest_out))
 
     def merged(chunk):
         splits = 2 if paired else 1
@@ -600,7 +588,10 @@
             total = lax.psum_scatter(partial[0], "tp", scatter_dimension=1, tiled=True)
         return total.reshape(groups, sides, 1, each, -1)
 
-    mixed = [summed(merged(0))]
+    partial = merged(0)
+    own_part[1], guest_out, partial = tied((own_part[1], guest_out, partial))
+    guest_part.append(exchange(guest_out))
+    mixed = [summed(partial)]
     guest_part[1], mixed = tied((guest_part[1], mixed))
     mixed.append(summed(merged(1)))
     return jnp.concatenate(mixed, axis=2).reshape(groups, shard_rows, -1)

time: 327 us -> 324 us (level)
  transfers between devices with their start and end apart: 13 -> 13, of which waited for: 10 -> 9; matrix products, arithmetic and copies ran while one was open for 4% -> 4% of each run, Pallas kernels for 44% -> 44%
where the time goes in v2:
time: 324 us; the launch traced here: 323 us
  Pallas kernels  155 us (48%)
  waiting for transfers between devices  82.4 us (25%)
  starting transfers between devices  59.9 us (18%)
  other arithmetic  15.2 us (5%)
  local copies, waits for them, and re-layouts  7.88 us (2%)
    pallas_call x4, Pallas kernels, attend(): pl.pallas_call(functools.partial(attend_kernel, causal, chunk, chunks, ro...  78.2 us
    all_to_all x7, starting transfers between devices, exchange(): return lax.all_to_all(value, 'grp', split_axis=0, concat_axis=0, tiled=True)  50.5 us
    ppermute x2, waiting for transfers between devices, summed(): arrived = lax.ppermute(theirs, 'tp', neighbour).astype(jnp.float32)  47.4 us
    pallas_call x5, Pallas kernels, project(): pl.pallas_call(functools.partial(project_kernel, turned, block // HEAD_DI...  43.7 us
    ppermute x4, waiting for transfers between devices, with_other(): return [arrived, lax.ppermute(arrived, 'tp', neighbour)]  29.5 us
    pallas_call x2, Pallas kernels, merge(): pl.pallas_call(functools.partial(merge_kernel, groups, heads), grid_spec=...  16.5 us
    pallas_call x1, Pallas kernels, replace_rows(): pl.pallas_call(functools.partial(replace_kernel, block), grid=(2, rows //...  10.9 us
  transfers between devices with their start and end apart: 13, of which 9 were waited for; matrix products, arithmetic and copies ran while one was open for 4% of the time, Pallas kernels for 44%

profile of v2, /device:TPU:0, one launch (start us, length us, event | category | flops | bytes accessed | tf_op | source)
XLA Modules:
  0.0 322.9 jit_solution(11157311823495457547)
XLA Ops:
  0.0 5.3 %deal.1 = (bf16[16,16,2048]{2,1,0:T(8,128)(2,1)}, bf16[16,16,2048]{2,1,0:T(8,128)(2,1)}, bf16[16,32,2048]{2,1,0:T(8,128)(2,1)}) custom-call(s32[16]{0:T(128)} %order_ref.1, s32[1]{0:T(128)} %bitcast.tp_ref, bf16[16,64,2048]{2,1,0:T(8,128)(2,1)} %x_ref.1), custom_call_target="tpu_custom_call" | custom-call | tf_op jit(solution)/shard_map/deal/pallas_call | solution.py:63
  5.3 7.5 %all-to-all-start = ((bf16[16,16,2048]{2,1,0:T(8,128)(2,1)}), bf16[16,16,2048]{2,1,0:T(8,128)(2,1)S(1)}, u32[]{:S(2)}, u32[]{:S(2)}) async-start(bf16[16,16,2048]{2,1,0:T(8,128)(2,1)} %get-tuple-element.60), calls=%async_computation | async-start | bytes 2097152 | tf_op jit(solution)/shard_map/all_to_all | solution.py:449
  16.4 3.7 %fusion.6 = (f32[1024,64]{1,0:T(8,128)S(1)}, f32[1024,64]{1,0:T(8,128)S(1)}, f32[1024,64]{1,0:T(8,128)S(1)}, f32[1024,64]{1,0:T(8,128)S(1)}, f32[1024,64]{1,0:T(8,128)S(1)}, /*index=5*/f32[1024,64]{1,0:T(8,128)S(1)}) fusion(f32[64]{0:T(128)S(1)} %multiply_exponential_fusion, f32[1024]{0:T(1024)S(1)} %convert_element_type.68, f32[1024]{0:T(1024)S(1)} %convert_element_type.65), kind=kLoop, calls=%fused_computation.21 | loop fusion | flops 262144 | bytes 1581312 | tf_op jit(solution)/shard_map/neg | solution.py:42
  27.5 6.8 %project.5 = (bf16[256,1024]{1,0:T(8,128)(2,1)}, bf16[256,1024]{1,0:T(8,128)(2,1)}) custom-call(s32[1]{0:T(128)} %bitcast.tp_ref, bf16[256,2048]{1,0:T(8,128)(2,1)} %fusion.4.refs_0_, f32[256,128]{1,0:T(8,128)} %get-tuple-element.135.refs_1_, f32[256,128]{1,0:T(8,128)} %get-tuple-element.136.refs_2_, bf16[2048,1024]{1,0:T(8,128)(2,1)} %refs_5_.3, ...), custom_call_target="tpu_custom_call" | custom-call | flops 2147483648 | bytes 10485760 | tf_op jit(solution)/shard_map/project/pallas_call | solution.py:121
  35.7 6.9 %all-to-all-start.1 = ((bf16[16,16,2048]{2,1,0:T(8,128)(2,1)}), bf16[16,16,2048]{2,1,0:T(8,128)(2,1)S(1)}, u32[]{:S(2)}, u32[]{:S(2)}) async-start(bf16[16,16,2048]{2,1,0:T(8,128)(2,1)} %get-tuple-element.64), calls=%async_computation.1 | async-start | bytes 2097152 | tf_op jit(solution)/shard_map/all_to_all | solution.py:449
  42.6 1.6 collective-permute-start
  44.2 10.9 %replace_rows.1.k_ref.v_ref = bf16[2,2048,1024]{2,1,0:T(8,128)(2,1)} custom-call(s32[1,256]{1,0:T(1,128)} %index_ref.1, bf16[1,2,2048,1024]{3,2,1,0:T(8,128)(2,1)} %cache_ref.1, bf16[256,1024]{1,0:T(8,128)(2,1)} %get-tuple-element.65.keys_ref, bf16[256,1024]{1,0:T(8,128)(2,1)} %get-tuple-element.66.values_ref), custom_call_target="tpu_custom_call" | custom-call | flops 2147483648 | bytes 20971520 | tf_op jit(solution)/shard_map/replace_rows/pallas_call | solution.py:166
  55.1 13.0 %collective-permute-done.refs_1_ = bf16[16,16,2048]{2,1,0:T(8,128)(2,1)S(1)} collective-permute-done((bf16[16,16,2048]{2,1,0:T(8,128)(2,1)S(1)}, bf16[16,16,2048]{2,1,0:T(8,128)(2,1)S(1)}, u32[]{:S(2)}, u32[]{:S(2)}) %collective-permute-start) | collective-permute-done | bytes 1048608 | tf_op jit(solution)/shard_map/ppermute | solution.py:500
  69.4 5.8 %all-to-all-start.2 = ((bf16[16,32,2048]{2,1,0:T(8,128)(2,1)}), bf16[16,32,2048]{2,1,0:T(8,128)(2,1)S(1)}, u32[]{:S(2)}, u32[]{:S(2)}) async-start(bf16[16,32,2048]{2,1,0:T(8,128)(2,1)} %get-tuple-element.69), calls=%async_computation.2 | async-start | bytes 4194304 | tf_op jit(solution)/shard_map/all_to_all | solution.py:449
  75.2 1.6 collective-permute-start.1
  76.7 11.8 %project.6 = (bf16[512,1024]{1,0:T(8,128)(2,1)}, bf16[512,1024]{1,0:T(8,128)(2,1)}, bf16[512,1024]{1,0:T(8,128)(2,1)}) custom-call(s32[1]{0:T(128)} %bitcast.tp_ref, bf16[16,16,2048]{2,1,0:T(8,128)(2,1)} %copy-done.8, bf16[16,16,2048]{2,1,0:T(8,128)(2,1)} %copy-done.14, f32[1024,128]{1,0:T(8,128)} %pad_maximum_fusion.1.refs_2_, ...), custom_call_target="tpu_custom_call" | custom-call | flops 6442450944 | bytes 17825792 | tf_op jit(solution)/shard_map/project/pallas_call | solution.py:121
  88.5 12.4 %collective-permute-done.1.refs_1_ = bf16[16,16,2048]{2,1,0:T(8,128)(2,1)S(1)} collective-permute-done((bf16[16,16,2048]{2,1,0:T(8,128)(2,1)}, bf16[16,16,2048]{2,1,0:T(8,128)(2,1)S(1)}, u32[]{:S(2)}, u32[]{:S(2)}) %collective-permute-start.1) | collective-permute-done | bytes 1048608 | tf_op jit(solution)/shard_map/ppermute | solution.py:500
  101.9 11.8 %project.7 = (bf16[512,1024]{1,0:T(8,128)(2,1)}, bf16[512,1024]{1,0:T(8,128)(2,1)}, bf16[512,1024]{1,0:T(8,128)(2,1)}) custom-call(s32[1]{0:T(128)} %bitcast.tp_ref, bf16[16,16,2048]{2,1,0:T(8,128)(2,1)} %copy-done.9, bf16[16,16,2048]{2,1,0:T(8,128)(2,1)} %copy-done.16, f32[1024,128]{1,0:T(8,128)} %pad_maximum_fusion.1.refs_2_, ...), custom_call_target="tpu_custom_call" | custom-call | flops 6442450944 | bytes 17825792 | tf_op jit(solution)/shard_map/project/pallas_call | solution.py:121
  113.6 2.6 all-to-all-done.2
  118.9 22.2 %attend_own.2 = bf16[512,1152]{1,0:T(8,128)(2,1)} custom-call(s32[1]{0:T(128)} %get-tuple-element.133.count_ref, bf16[512,1024]{1,0:T(8,128)(2,1)} %get-tuple-element.81.q_ref, bf16[2,2048,1024]{2,1,0:T(8,128)(2,1)} %replace_rows.1.k_ref.v_ref, bf16[2,2048,1024]{2,1,0:T(8,128)(2,1)} %replace_rows.1.k_ref.v_ref, bf16[512,1024]{1,0:T(8,128)(2,1)} %get-tuple-element.83.refs_0_, ...), custom_call_target="tpu_custom_call" | custom-call | flops 21474836480 | bytes 10485760 | tf_op jit(solution)/shard_map/attend_own/pallas_call | solution.py:330
  141.1 2.1 collective-permute-done.2.refs_1_
  144.2 10.7 %all-to-all-start.3 = ((bf16[16,32,1152]{2,1,0:T(8,128)(2,1)}), bf16[16,32,1152]{2,1,0:T(8,128)(2,1)S(1)}, u32[]{:S(2)}, u32[]{:S(2)}) async-start(bf16[16,32,1152]{2,1,0:T(8,128)(2,1)} %bitcast.36), calls=%async_computation.3 | async-start | bytes 2359296 | tf_op jit(solution)/shard_map/all_to_all | solution.py:449
  155.0 6.7 %project.8.q_ref = bf16[512,1024]{1,0:T(8,128)(2,1)} custom-call(s32[1]{0:T(128)} %bitcast.tp_ref, bf16[16,16,2048]{2,1,0:T(8,128)(2,1)} %copy-done.6, bf16[16,16,2048]{2,1,0:T(8,128)(2,1)} %copy-done.7, f32[1024,128]{1,0:T(8,128)} %pad_maximum_fusion.3.refs_2_, f32[1024,128]{1,0:T(8,128)} %pad_maximum_fusion.4.refs_3_, bf16[2048,1024]{1,0:T(8,128)(2,1)} %refs_4_.9), custom_call_target="tpu_custom_call" | custom-call | flops 2147483648 | bytes 7340032 | tf_op jit(solution)/shard_map/project/pallas_call | solution.py:121
  161.7 16.9 %attend_guest.2 = bf16[512,1152]{1,0:T(8,128)(2,1)} custom-call(s32[1]{0:T(128)} %get-tuple-element.129.count_ref, bf16[512,1024]{1,0:T(8,128)(2,1)} %project.8.q_ref, bf16[1,2,2048,1024]{3,2,1,0:T(8,128)(2,1)} %v_ref.3, bf16[1,2,2048,1024]{3,2,1,0:T(8,128)(2,1)} %v_ref.3), custom_call_target="tpu_custom_call" | custom-call | flops 17179869184 | bytes 10485760 | tf_op jit(solution)/shard_map/attend_guest/pallas_call | solution.py:330
  180.1 7.5 %all-to-all-start.4 = ((bf16[16,32,1152]{2,1,0:T(8,128)(2,1)}), bf16[16,32,1152]{2,1,0:T(8,128)(2,1)S(1)}, u32[]{:S(2)}, u32[]{:S(2)}) async-start(bf16[16,32,1152]{2,1,0:T(8,128)(2,1)} %bitcast.34), calls=%async_computation.4 | async-start | bytes 2359296 | tf_op jit(solution)/shard_map/all_to_all | solution.py:449
  189.2 22.2 %attend_own.3 = bf16[512,1152]{1,0:T(8,128)(2,1)} custom-call(s32[1]{0:T(128)} %get-tuple-element.133.count_ref, bf16[512,1024]{1,0:T(8,128)(2,1)} %get-tuple-element.98.q_ref, bf16[2,2048,1024]{2,1,0:T(8,128)(2,1)} %replace_rows.1.k_ref.v_ref, bf16[2,2048,1024]{2,1,0:T(8,128)(2,1)} %replace_rows.1.k_ref.v_ref, bf16[512,1024]{1,0:T(8,128)(2,1)} %get-tuple-element.83.refs_0_, ...), custom_call_target="tpu_custom_call" | custom-call | flops 21474836480 | bytes 10485760 | tf_op jit(solution)/shard_map/attend_own/pallas_call | solution.py:330
  211.4 1.9 collective-permute-done.3.refs_1_
  213.3 6.9 %all-to-all-start.5 = ((bf16[16,32,1152]{2,1,0:T(8,128)(2,1)}), bf16[16,32,1152]{2,1,0:T(8,128)(2,1)S(1)}, u32[]{:S(2)}, u32[]{:S(2)}) async-start(bf16[16,32,1152]{2,1,0:T(8,128)(2,1)} %bitcast.33), calls=%async_computation.5 | async-start | bytes 2359296 | tf_op jit(solution)/shard_map/all_to_all | solution.py:449
  220.9 8.2 %merge.2 = (bf16[512,1024]{1,0:T(8,128)(2,1)}, bf16[512,1024]{1,0:T(8,128)(2,1)}) custom-call(s32[16]{0:T(128)} %select_reduce_fusion.inverse_ref, s32[1]{0:T(128)} %bitcast.tp_ref, bf16[16,32,1152]{2,1,0:T(8,128)(2,1)} %copy-done.2, bf16[16,32,1152]{2,1,0:T(8,128)(2,1)} %copy-done.3, bf16[1024,2048]{1,0:T(8,128)(2,1)} %w_ref.3), custom_call_target="tpu_custom_call" | custom-call | flops 1073741824 | bytes 1048576 | tf_op jit(solution)/shard_map/merge/pallas_call | solution.py:425
  229.2 6.7 %project.9.q_ref = bf16[512,1024]{1,0:T(8,128)(2,1)} custom-call(s32[1]{0:T(128)} %bitcast.tp_ref, bf16[16,16,2048]{2,1,0:T(8,128)(2,1)} %get-tuple-element.101.refs_0_, bf16[16,16,2048]{2,1,0:T(8,128)(2,1)} %collective-permute-done.3.refs_1_, f32[1024,128]{1,0:T(8,128)} %pad_maximum_fusion.3.refs_2_, f32[1024,128]{1,0:T(8,128)} %pad_maximum_fusion.4.refs_3_, ...), custom_call_target="tpu_custom_call" | custom-call | flops 2147483648 | bytes 7340032 | tf_op jit(solution)/shard_map/project/pallas_call | solution.py:121
  235.9 17.0 %attend_guest.3 = bf16[512,1152]{1,0:T(8,128)(2,1)} custom-call(s32[1]{0:T(128)} %get-tuple-element.129.count_ref, bf16[512,1024]{1,0:T(8,128)(2,1)} %project.9.q_ref, bf16[1,2,2048,1024]{3,2,1,0:T(8,128)(2,1)} %v_ref.3, bf16[1,2,2048,1024]{3,2,1,0:T(8,128)(2,1)} %v_ref.3), custom_call_target="tpu_custom_call" | custom-call | flops 17179869184 | bytes 10485760 | tf_op jit(solution)/shard_map/attend_guest/pallas_call | solution.py:330
  252.8 5.2 %all-to-all-start.6 = ((bf16[16,32,1152]{2,1,0:T(8,128)(2,1)}), bf16[16,32,1152]{2,1,0:T(8,128)(2,1)S(1)}, u32[]{:S(2)}, u32[]{:S(2)}) async-start(bf16[16,32,1152]{2,1,0:T(8,128)(2,1)} %bitcast.35), calls=%async_computation.6 | async-start | bytes 2359296 | tf_op jit(solution)/shard_map/all_to_all | solution.py:449
  259.7 24.0 %collective-permute-done.4 = bf16[512,1024]{1,0:T(8,128)(2,1)S(1)} collective-permute-done((bf16[512,1024]{1,0:T(8,128)(2,1)S(1)}, bf16[512,1024]{1,0:T(8,128)(2,1)S(1)}, u32[]{:S(2)}, u32[]{:S(2)}) %collective-permute-start.4) | collective-permute-done | bytes 1048608 | tf_op jit(solution)/shard_map/ppermute | solution.py:585
  283.6 1.6 add_convert_fusion.1
  286.3 8.3 %merge.3 = (bf16[512,1024]{1,0:T(8,128)(2,1)}, bf16[512,1024]{1,0:T(8,128)(2,1)}) custom-call(s32[16]{0:T(128)} %select_reduce_fusion.inverse_ref, s32[1]{0:T(128)} %bitcast.tp_ref, bf16[16,32,1152]{2,1,0:T(8,128)(2,1)} %copy-done.1, bf16[16,32,1152]{2,1,0:T(8,128)(2,1)} %copy-done.4, bf16[1024,2048]{1,0:T(8,128)(2,1)} %w_ref.3), custom_call_target="tpu_custom_call" | custom-call | flops 1073741824 | bytes 1048576 | tf_op jit(solution)/shard_map/merge/pallas_call | solution.py:425
  296.1 23.4 %collective-permute-done.5 = bf16[512,1024]{1,0:T(8,128)(2,1)S(1)} collective-permute-done((bf16[512,1024]{1,0:T(8,128)(2,1)}, bf16[512,1024]{1,0:T(8,128)(2,1)S(1)}, u32[]{:S(2)}, u32[]{:S(2)}) %collective-permute-start.5) | collective-permute-done | bytes 1048608 | tf_op jit(solution)/shard_map/ppermute | solution.py:585
  319.5 1.6 add_convert_fusion
  (66 shorter events, 25.3 us)
Async XLA Ops:
  5.3 7.5 %copy-start.11 = (s32[16]{0:T(128)S(1)}, s32[16]{0:T(128)}, u32[]{:S(2)}) copy-start(s32[16]{0:T(128)} %param.22) | copy-start | bytes 196
  5.3 7.5 %copy-start.12 = (s32[16]{0:T(128)S(1)}, s32[16]{0:T(128)}, u32[]{:S(2)}) copy-start(s32[16]{0:T(128)} %param.21) | copy-start | bytes 196
  5.3 30.4 %all-to-all-start = ((bf16[16,16,2048]{2,1,0:T(8,128)(2,1)}), bf16[16,16,2048]{2,1,0:T(8,128)(2,1)S(1)}, u32[]{:S(2)}, u32[]{:S(2)}) async-start(bf16[16,16,2048]{2,1,0:T(8,128)(2,1)} %get-tuple-element.60), calls=%async_computation | async-start | bytes 2097152 | tf_op jit(solution)/shard_map/all_to_all | solution.py:449
  16.4 4.7 %copy-start.10 = (s32[1,256]{1,0:T(1,128)S(1)}, s32[1,256]{1,0:T(1,128)}, u32[]{:S(2)}) copy-start(s32[1,256]{1,0:T(1,128)} %index_ref.1) | copy-start | bytes 3076
  22.5 3.0 copy-start
  35.7 19.4 %copy-start.8 = (bf16[16,16,2048]{2,1,0:T(8,128)(2,1)}, bf16[16,16,2048]{2,1,0:T(8,128)(2,1)S(1)}, u32[]{:S(2)}) copy-start(bf16[16,16,2048]{2,1,0:T(8,128)(2,1)S(1)} %all-to-all-done.refs_0_) | copy-start | bytes 3145732
  35.7 32.4 %all-to-all-start.1 = ((bf16[16,16,2048]{2,1,0:T(8,128)(2,1)}), bf16[16,16,2048]{2,1,0:T(8,128)(2,1)S(1)}, u32[]{:S(2)}, u32[]{:S(2)}) async-start(bf16[16,16,2048]{2,1,0:T(8,128)(2,1)} %get-tuple-element.64), calls=%async_computation.1 | async-start | bytes 2097152 | tf_op jit(solution)/shard_map/all_to_all | solution.py:449
  42.6 25.5 %collective-permute-start = (bf16[16,16,2048]{2,1,0:T(8,128)(2,1)S(1)}, bf16[16,16,2048]{2,1,0:T(8,128)(2,1)S(1)}, u32[]{:S(2)}, u32[]{:S(2)}) collective-permute-start(bf16[16,16,2048]{2,1,0:T(8,128)(2,1)S(1)} %all-to-all-done.refs_0_), channel_id=1, source_target_pairs={{0,1},{1,0},{2,3},{3,2},{4,5},{5,4},{6,7},{7,6},{8,9},{9,8},{10,11... | collective-permute-start | bytes 3145736 | tf_op jit(solution)/shard_map/ppermute | solution.py:500
  68.1 1.0 copy-start.14
  68.1 1.3 copy-start.9
  69.4 46.9 %all-to-all-start.2 = ((bf16[16,32,2048]{2,1,0:T(8,128)(2,1)}), bf16[16,32,2048]{2,1,0:T(8,128)(2,1)S(1)}, u32[]{:S(2)}, u32[]{:S(2)}) async-start(bf16[16,32,2048]{2,1,0:T(8,128)(2,1)} %get-tuple-element.69), calls=%async_computation.2 | async-start | bytes 4194304 | tf_op jit(solution)/shard_map/all_to_all | solution.py:449
  75.2 25.8 %collective-permute-start.1 = (bf16[16,16,2048]{2,1,0:T(8,128)(2,1)}, bf16[16,16,2048]{2,1,0:T(8,128)(2,1)S(1)}, u32[]{:S(2)}, u32[]{:S(2)}) collective-permute-start(bf16[16,16,2048]{2,1,0:T(8,128)(2,1)} %copy-done.9), channel_id=1, source_target_pairs={{0,1},{1,0},{2,3},{3,2},{4,5},{5,4},{6,7},{7,6},{8,9},{9,8},{10,11... | collective-permute-start | bytes 3145736 | tf_op jit(solution)/shard_map/ppermute | solution.py:500
  100.9 1.0 copy-start.16
  117.4 23.7 %copy-start.6 = (bf16[16,16,2048]{2,1,0:T(8,128)(2,1)}, bf16[16,16,2048]{2,1,0:T(8,128)(2,1)S(1)}, u32[]{:S(2)}) copy-start(bf16[16,16,2048]{2,1,0:T(8,128)(2,1)S(1)} %get-tuple-element.92.refs_0_) | copy-start | bytes 3145732
  117.4 25.8 %collective-permute-start.2 = (bf16[16,16,2048]{2,1,0:T(8,128)(2,1)S(1)}, bf16[16,16,2048]{2,1,0:T(8,128)(2,1)S(1)}, u32[]{:S(2)}, u32[]{:S(2)}) collective-permute-start(bf16[16,16,2048]{2,1,0:T(8,128)(2,1)S(1)} %get-tuple-element.92.refs_0_), channel_id=1, source_target_pairs={{0,1},{1,0},{2,3},{3,2},{4,5},{5,4},{6,7},{7,6},{8,9},{9,8},{10,11... | collective-permute-start | bytes 3145736 | tf_op jit(solution)/shard_map/ppermute | solution.py:500
  143.2 1.0 copy-start.7
  144.2 35.9 %all-to-all-start.3 = ((bf16[16,32,1152]{2,1,0:T(8,128)(2,1)}), bf16[16,32,1152]{2,1,0:T(8,128)(2,1)S(1)}, u32[]{:S(2)}, u32[]{:S(2)}) async-start(bf16[16,32,1152]{2,1,0:T(8,128)(2,1)} %bitcast.36), calls=%async_computation.3 | async-start | bytes 2359296 | tf_op jit(solution)/shard_map/all_to_all | solution.py:449
  178.6 9.0 %copy-start.5 = (bf16[16,16,2048]{2,1,0:T(8,128)(2,1)S(1)}, bf16[16,16,2048]{2,1,0:T(8,128)(2,1)}, u32[]{:S(2)}) copy-start(bf16[16,16,2048]{2,1,0:T(8,128)(2,1)} %get-tuple-element.101.refs_0_) | copy-start | bytes 3145732
  180.1 31.3 %copy-start.2 = (bf16[16,32,1152]{2,1,0:T(8,128)(2,1)}, bf16[16,32,1152]{2,1,0:T(8,128)(2,1)S(1)}, u32[]{:S(2)}) copy-start(bf16[16,32,1152]{2,1,0:T(8,128)(2,1)S(1)} %all-to-all-done.3.own_ref) | copy-start | bytes 3538948
  180.1 33.2 %all-to-all-start.4 = ((bf16[16,32,1152]{2,1,0:T(8,128)(2,1)}), bf16[16,32,1152]{2,1,0:T(8,128)(2,1)S(1)}, u32[]{:S(2)}, u32[]{:S(2)}) async-start(bf16[16,32,1152]{2,1,0:T(8,128)(2,1)} %bitcast.34), calls=%async_computation.4 | async-start | bytes 2359296 | tf_op jit(solution)/shard_map/all_to_all | solution.py:449
  187.6 25.7 %collective-permute-start.3 = (bf16[16,16,2048]{2,1,0:T(8,128)(2,1)S(1)}, bf16[16,16,2048]{2,1,0:T(8,128)(2,1)}, u32[]{:S(2)}, u32[]{:S(2)}) collective-permute-start(bf16[16,16,2048]{2,1,0:T(8,128)(2,1)S(1)} %copy-done.5), channel_id=1, source_target_pairs={{0,1},{1,0},{2,3},{3,2},{4,5},{5,4},{6,7},{7,6},{8,9},{9,8},{10,11... | collective-permute-start | bytes 3145736 | tf_op jit(solution)/shard_map/ppermute | solution.py:500
  211.4 8.9 %copy-start.13 = (s32[16]{0:T(128)S(1)}, s32[16]{0:T(128)}, u32[]{:S(2)}) copy-start(s32[16]{0:T(128)} %order_ref.1) | copy-start | bytes 196
  213.3 7.6 %copy-start.3 = (bf16[16,32,1152]{2,1,0:T(8,128)(2,1)}, bf16[16,32,1152]{2,1,0:T(8,128)(2,1)S(1)}, u32[]{:S(2)}) copy-start(bf16[16,32,1152]{2,1,0:T(8,128)(2,1)S(1)} %all-to-all-done.4.guest_ref) | copy-start | bytes 3538948
  213.3 39.5 %all-to-all-start.5 = ((bf16[16,32,1152]{2,1,0:T(8,128)(2,1)}), bf16[16,32,1152]{2,1,0:T(8,128)(2,1)S(1)}, u32[]{:S(2)}, u32[]{:S(2)}) async-start(bf16[16,32,1152]{2,1,0:T(8,128)(2,1)} %bitcast.33), calls=%async_computation.5 | async-start | bytes 2359296 | tf_op jit(solution)/shard_map/all_to_all | solution.py:449
  252.8 5.3 %copy-start.15 = (bf16[512,1024]{1,0:T(8,128)(2,1)S(1)}, bf16[512,1024]{1,0:T(8,128)(2,1)}, u32[]{:S(2)}) copy-start(bf16[512,1024]{1,0:T(8,128)(2,1)} %get-tuple-element.109) | copy-start | bytes 3145732
  252.8 32.4 %copy-start.1 = (bf16[16,32,1152]{2,1,0:T(8,128)(2,1)}, bf16[16,32,1152]{2,1,0:T(8,128)(2,1)S(1)}, u32[]{:S(2)}) copy-start(bf16[16,32,1152]{2,1,0:T(8,128)(2,1)S(1)} %all-to-all-done.5.own_ref) | copy-start | bytes 3538948
  252.8 32.5 %all-to-all-start.6 = ((bf16[16,32,1152]{2,1,0:T(8,128)(2,1)}), bf16[16,32,1152]{2,1,0:T(8,128)(2,1)S(1)}, u32[]{:S(2)}, u32[]{:S(2)}) async-start(bf16[16,32,1152]{2,1,0:T(8,128)(2,1)} %bitcast.35), calls=%async_computation.6 | async-start | bytes 2359296 | tf_op jit(solution)/shard_map/all_to_all | solution.py:449
  258.1 25.6 %collective-permute-start.4 = (bf16[512,1024]{1,0:T(8,128)(2,1)S(1)}, bf16[512,1024]{1,0:T(8,128)(2,1)S(1)}, u32[]{:S(2)}, u32[]{:S(2)}) collective-permute-start(bf16[512,1024]{1,0:T(8,128)(2,1)S(1)} %copy-done.15), channel_id=1, source_target_pairs={{0,1},{1,0},{2,3},{3,2},{4,5},{5,4},{6,7},{7,6},{8,9},{9,8},{10,11... | collective-permute-start | bytes 3145736 | tf_op jit(solution)/shard_map/ppermute | solution.py:585
  285.3 1.0 copy-start.4
  294.6 24.9 %collective-permute-start.5 = (bf16[512,1024]{1,0:T(8,128)(2,1)}, bf16[512,1024]{1,0:T(8,128)(2,1)S(1)}, u32[]{:S(2)}, u32[]{:S(2)}) collective-permute-start(bf16[512,1024]{1,0:T(8,128)(2,1)} %get-tuple-element.114), channel_id=1, source_target_pairs={{0,1},{1,0},{2,3},{3,2},{4,5},{5,4},{6,7},{7,6},{8,9},{9,8},{10,11... | collective-permute-start | bytes 3145736 | tf_op jit(solution)/shard_map/ppermute | solution.py:585

commit v3 on v2

--- a/solution.py
+++ b/solution.py
@@ -579,21 +579,22 @@
         splits = 2 if paired else 1
         return merge(inverse, tp_index, splits, own_part[chunk], guest_part[chunk], w_out)
 
-    def summed(partial):
+    def summed(mine, arrived):
+        total = (mine.astype(jnp.float32) + arrived.astype(jnp.float32)).astype(jnp.bfloat16)
+        return total.reshape(groups, sides, 1, each, -1)
+
+    def swapped(partial):
         if paired:
-            theirs, mine = partial
-            arrived = lax.ppermute(theirs, "tp", neighbour).astype(jnp.float32)
-            total = (mine.astype(jnp.float32) + arrived).astype(jnp.bfloat16)
-        else:
-            total = lax.psum_scatter(partial[0], "tp", scatter_dimension=1, tiled=True)
-        return total.reshape(groups, sides, 1, each, -1)
+            return partial[1], lax.ppermute(partial[0], "tp", neighbour)
+        total = lax.psum_scatter(partial[0], "tp", scatter_dimension=1, tiled=True)
+        return total, jnp.zeros_like(total)
 
     partial = merged(0)
     own_part[1], guest_out, partial = tied((own_part[1], guest_out, partial))
     guest_part.append(exchange(guest_out))
-    mixed = [summed(partial)]
-    guest_part[1], mixed = tied((guest_part[1], mixed))
-    mixed.append(summed(merged(1)))
+    terms = swapped(partial)
+    guest_part[1], terms = tied((guest_part[1], terms))
+    mixed = [summed(*terms), summed(*swapped(merged(1)))]
     return jnp.concatenate(mixed, axis=2).reshape(groups, shard_rows, -1)
 
 

time: 324 us -> 322 us (level)
  no operation moved by 1% of the time
where the time goes in v3:
time: 322 us; the launch traced here: 321 us
  Pallas kernels  155 us (48%)
  waiting for transfers between devices  81.7 us (25%)
  starting transfers between devices  60.7 us (19%)
  other arithmetic  14 us (4%)
  local copies, waits for them, and re-layouts  6.93 us (2%)
    pallas_call x4, Pallas kernels, attend(): pl.pallas_call(functools.partial(attend_kernel, causal, chunk, chunks, ro...  78.2 us
    all_to_all x7, starting transfers between devices, exchange(): return lax.all_to_all(value, 'grp', split_axis=0, concat_axis=0, tiled=True)  51.3 us
    ppermute x2, waiting for transfers between devices, swapped(): return (partial[1], lax.ppermute(partial[0], 'tp', neighbour))  46.4 us
    pallas_call x5, Pallas kernels, project(): pl.pallas_call(functools.partial(project_kernel, turned, block // HEAD_DI...  43.7 us
    ppermute x4, waiting for transfers between devices, with_other(): return [arrived, lax.ppermute(arrived, 'tp', neighbour)]  29.7 us
    pallas_call x2, Pallas kernels, merge(): pl.pallas_call(functools.partial(merge_kernel, groups, heads), grid_spec=...  16.5 us
    pallas_call x1, Pallas kernels, replace_rows(): pl.pallas_call(functools.partial(replace_kernel, block), grid=(2, rows //...  10.9 us
  transfers between devices with their start and end apart: 13, of which 9 were waited for; matrix products, arithmetic and copies ran while one was open for 4% of the time, Pallas kernels for 44%

profile of v3, /device:TPU:0, one launch (start us, length us, event | category | flops | bytes accessed | tf_op | source)
XLA Modules:
  0.0 320.7 jit_solution(16631584368012455702)
XLA Ops:
  0.0 5.3 %deal.1 = (bf16[16,16,2048]{2,1,0:T(8,128)(2,1)}, bf16[16,16,2048]{2,1,0:T(8,128)(2,1)}, bf16[16,32,2048]{2,1,0:T(8,128)(2,1)}) custom-call(s32[16]{0:T(128)} %order_ref.1, s32[1]{0:T(128)} %bitcast.tp_ref, bf16[16,64,2048]{2,1,0:T(8,128)(2,1)} %x_ref.1), custom_call_target="tpu_custom_call" | custom-call | tf_op jit(solution)/shard_map/deal/pallas_call | solution.py:63
  5.3 7.5 %all-to-all-start = ((bf16[16,16,2048]{2,1,0:T(8,128)(2,1)}), bf16[16,16,2048]{2,1,0:T(8,128)(2,1)S(1)}, u32[]{:S(2)}, u32[]{:S(2)}) async-start(bf16[16,16,2048]{2,1,0:T(8,128)(2,1)} %get-tuple-element.61), calls=%async_computation | async-start | bytes 2097152 | tf_op jit(solution)/shard_map/all_to_all | solution.py:449
  16.4 3.7 %fusion.6 = (f32[1024,64]{1,0:T(8,128)S(1)}, f32[1024,64]{1,0:T(8,128)S(1)}, f32[1024,64]{1,0:T(8,128)S(1)}, f32[1024,64]{1,0:T(8,128)S(1)}, f32[1024,64]{1,0:T(8,128)S(1)}, /*index=5*/f32[1024,64]{1,0:T(8,128)S(1)}) fusion(f32[64]{0:T(128)S(1)} %multiply_exponential_fusion, f32[1024]{0:T(1024)S(1)} %convert_element_type.68, f32[1024]{0:T(1024)S(1)} %convert_element_type.65), kind=kLoop, calls=%fused_computation.21 | loop fusion | flops 262144 | bytes 1581312 | tf_op jit(solution)/shard_map/neg | solution.py:42
  27.5 6.8 %project.5 = (bf16[256,1024]{1,0:T(8,128)(2,1)}, bf16[256,1024]{1,0:T(8,128)(2,1)}) custom-call(s32[1]{0:T(128)} %bitcast.tp_ref, bf16[256,2048]{1,0:T(8,128)(2,1)} %fusion.4.refs_0_, f32[256,128]{1,0:T(8,128)} %get-tuple-element.137.refs_1_, f32[256,128]{1,0:T(8,128)} %get-tuple-element.138.refs_2_, bf16[2048,1024]{1,0:T(8,128)(2,1)} %refs_5_.3, ...), custom_call_target="tpu_custom_call" | custom-call | flops 2147483648 | bytes 10485760 | tf_op jit(solution)/shard_map/project/pallas_call | solution.py:121
  35.7 6.9 %all-to-all-start.1 = ((bf16[16,16,2048]{2,1,0:T(8,128)(2,1)}), bf16[16,16,2048]{2,1,0:T(8,128)(2,1)S(1)}, u32[]{:S(2)}, u32[]{:S(2)}) async-start(bf16[16,16,2048]{2,1,0:T(8,128)(2,1)} %get-tuple-element.65), calls=%async_computation.1 | async-start | bytes 2097152 | tf_op jit(solution)/shard_map/all_to_all | solution.py:449
  42.6 1.6 collective-permute-start
  44.2 10.9 %replace_rows.1.k_ref.v_ref = bf16[2,2048,1024]{2,1,0:T(8,128)(2,1)} custom-call(s32[1,256]{1,0:T(1,128)} %index_ref.1, bf16[1,2,2048,1024]{3,2,1,0:T(8,128)(2,1)} %cache_ref.1, bf16[256,1024]{1,0:T(8,128)(2,1)} %get-tuple-element.66.keys_ref, bf16[256,1024]{1,0:T(8,128)(2,1)} %get-tuple-element.67.values_ref), custom_call_target="tpu_custom_call" | custom-call | flops 2147483648 | bytes 20971520 | tf_op jit(solution)/shard_map/replace_rows/pallas_call | solution.py:166
  55.1 13.0 %collective-permute-done.refs_1_ = bf16[16,16,2048]{2,1,0:T(8,128)(2,1)S(1)} collective-permute-done((bf16[16,16,2048]{2,1,0:T(8,128)(2,1)S(1)}, bf16[16,16,2048]{2,1,0:T(8,128)(2,1)S(1)}, u32[]{:S(2)}, u32[]{:S(2)}) %collective-permute-start) | collective-permute-done | bytes 1048608 | tf_op jit(solution)/shard_map/ppermute | solution.py:500
  69.4 5.8 %all-to-all-start.2 = ((bf16[16,32,2048]{2,1,0:T(8,128)(2,1)}), bf16[16,32,2048]{2,1,0:T(8,128)(2,1)S(1)}, u32[]{:S(2)}, u32[]{:S(2)}) async-start(bf16[16,32,2048]{2,1,0:T(8,128)(2,1)} %get-tuple-element.70), calls=%async_computation.2 | async-start | bytes 4194304 | tf_op jit(solution)/shard_map/all_to_all | solution.py:449
  75.2 1.6 collective-permute-start.1
  76.7 11.8 %project.6 = (bf16[512,1024]{1,0:T(8,128)(2,1)}, bf16[512,1024]{1,0:T(8,128)(2,1)}, bf16[512,1024]{1,0:T(8,128)(2,1)}) custom-call(s32[1]{0:T(128)} %bitcast.tp_ref, bf16[16,16,2048]{2,1,0:T(8,128)(2,1)} %copy-done.9, bf16[16,16,2048]{2,1,0:T(8,128)(2,1)} %copy-done.15, f32[1024,128]{1,0:T(8,128)} %pad_maximum_fusion.1.refs_2_, ...), custom_call_target="tpu_custom_call" | custom-call | flops 6442450944 | bytes 17825792 | tf_op jit(solution)/shard_map/project/pallas_call | solution.py:121
  88.5 12.4 %collective-permute-done.1.refs_1_ = bf16[16,16,2048]{2,1,0:T(8,128)(2,1)S(1)} collective-permute-done((bf16[16,16,2048]{2,1,0:T(8,128)(2,1)}, bf16[16,16,2048]{2,1,0:T(8,128)(2,1)S(1)}, u32[]{:S(2)}, u32[]{:S(2)}) %collective-permute-start.1) | collective-permute-done | bytes 1048608 | tf_op jit(solution)/shard_map/ppermute | solution.py:500
  101.9 11.8 %project.7 = (bf16[512,1024]{1,0:T(8,128)(2,1)}, bf16[512,1024]{1,0:T(8,128)(2,1)}, bf16[512,1024]{1,0:T(8,128)(2,1)}) custom-call(s32[1]{0:T(128)} %bitcast.tp_ref, bf16[16,16,2048]{2,1,0:T(8,128)(2,1)} %copy-done.10, bf16[16,16,2048]{2,1,0:T(8,128)(2,1)} %copy-done.16, f32[1024,128]{1,0:T(8,128)} %pad_maximum_fusion.1.refs_2_, ...), custom_call_target="tpu_custom_call" | custom-call | flops 6442450944 | bytes 17825792 | tf_op jit(solution)/shard_map/project/pallas_call | solution.py:121
  113.6 2.6 all-to-all-done.2
  119.0 22.2 %attend_own.2 = bf16[512,1152]{1,0:T(8,128)(2,1)} custom-call(s32[1]{0:T(128)} %get-tuple-element.135.count_ref, bf16[512,1024]{1,0:T(8,128)(2,1)} %get-tuple-element.82.q_ref, bf16[2,2048,1024]{2,1,0:T(8,128)(2,1)} %replace_rows.1.k_ref.v_ref, bf16[2,2048,1024]{2,1,0:T(8,128)(2,1)} %replace_rows.1.k_ref.v_ref, bf16[512,1024]{1,0:T(8,128)(2,1)} %get-tuple-element.84.refs_0_, ...), custom_call_target="tpu_custom_call" | custom-call | flops 21474836480 | bytes 10485760 | tf_op jit(solution)/shard_map/attend_own/pallas_call | solution.py:330
  141.1 2.4 collective-permute-done.2.refs_1_
  143.5 10.8 %all-to-all-start.3 = ((bf16[16,32,1152]{2,1,0:T(8,128)(2,1)}), bf16[16,32,1152]{2,1,0:T(8,128)(2,1)S(1)}, u32[]{:S(2)}, u32[]{:S(2)}) async-start(bf16[16,32,1152]{2,1,0:T(8,128)(2,1)} %bitcast.36), calls=%async_computation.3 | async-start | bytes 2359296 | tf_op jit(solution)/shard_map/all_to_all | solution.py:449
  154.3 6.7 %project.8.q_ref = bf16[512,1024]{1,0:T(8,128)(2,1)} custom-call(s32[1]{0:T(128)} %bitcast.tp_ref, bf16[16,16,2048]{2,1,0:T(8,128)(2,1)} %get-tuple-element.93.refs_0_, bf16[16,16,2048]{2,1,0:T(8,128)(2,1)} %copy-done.8, f32[1024,128]{1,0:T(8,128)} %pad_maximum_fusion.3.refs_2_, f32[1024,128]{1,0:T(8,128)} %pad_maximum_fusion.4.refs_3_, ...), custom_call_target="tpu_custom_call" | custom-call | flops 2147483648 | bytes 7340032 | tf_op jit(solution)/shard_map/project/pallas_call | solution.py:121
  161.0 16.9 %attend_guest.2 = bf16[512,1152]{1,0:T(8,128)(2,1)} custom-call(s32[1]{0:T(128)} %get-tuple-element.131.count_ref, bf16[512,1024]{1,0:T(8,128)(2,1)} %project.8.q_ref, bf16[1,2,2048,1024]{3,2,1,0:T(8,128)(2,1)} %v_ref.3, bf16[1,2,2048,1024]{3,2,1,0:T(8,128)(2,1)} %v_ref.3), custom_call_target="tpu_custom_call" | custom-call | flops 17179869184 | bytes 10485760 | tf_op jit(solution)/shard_map/attend_guest/pallas_call | solution.py:330
  179.4 7.5 %all-to-all-start.4 = ((bf16[16,32,1152]{2,1,0:T(8,128)(2,1)}), bf16[16,32,1152]{2,1,0:T(8,128)(2,1)S(1)}, u32[]{:S(2)}, u32[]{:S(2)}) async-start(bf16[16,32,1152]{2,1,0:T(8,128)(2,1)} %bitcast.34), calls=%async_computation.4 | async-start | bytes 2359296 | tf_op jit(solution)/shard_map/all_to_all | solution.py:449
  186.9 1.6 collective-permute-start.3
  188.5 22.2 %attend_own.3 = bf16[512,1152]{1,0:T(8,128)(2,1)} custom-call(s32[1]{0:T(128)} %get-tuple-element.135.count_ref, bf16[512,1024]{1,0:T(8,128)(2,1)} %get-tuple-element.99.q_ref, bf16[2,2048,1024]{2,1,0:T(8,128)(2,1)} %replace_rows.1.k_ref.v_ref, bf16[2,2048,1024]{2,1,0:T(8,128)(2,1)} %replace_rows.1.k_ref.v_ref, bf16[512,1024]{1,0:T(8,128)(2,1)} %get-tuple-element.84.refs_0_, ...), custom_call_target="tpu_custom_call" | custom-call | flops 21474836480 | bytes 10485760 | tf_op jit(solution)/shard_map/attend_own/pallas_call | solution.py:330
  210.6 1.9 collective-permute-done.3.refs_1_
  212.5 6.9 %all-to-all-start.5 = ((bf16[16,32,1152]{2,1,0:T(8,128)(2,1)}), bf16[16,32,1152]{2,1,0:T(8,128)(2,1)S(1)}, u32[]{:S(2)}, u32[]{:S(2)}) async-start(bf16[16,32,1152]{2,1,0:T(8,128)(2,1)} %bitcast.33), calls=%async_computation.5 | async-start | bytes 2359296 | tf_op jit(solution)/shard_map/all_to_all | solution.py:449
  220.2 8.2 %merge.2 = (bf16[512,1024]{1,0:T(8,128)(2,1)}, bf16[512,1024]{1,0:T(8,128)(2,1)}) custom-call(s32[16]{0:T(128)} %select_reduce_fusion.inverse_ref, s32[1]{0:T(128)} %bitcast.tp_ref, bf16[16,32,1152]{2,1,0:T(8,128)(2,1)} %copy-done.1, bf16[16,32,1152]{2,1,0:T(8,128)(2,1)} %copy-done.3, bf16[1024,2048]{1,0:T(8,128)(2,1)} %w_ref.3), custom_call_target="tpu_custom_call" | custom-call | flops 1073741824 | bytes 1048576 | tf_op jit(solution)/shard_map/merge/pallas_call | solution.py:425
  228.4 6.7 %project.9.q_ref = bf16[512,1024]{1,0:T(8,128)(2,1)} custom-call(s32[1]{0:T(128)} %bitcast.tp_ref, bf16[16,16,2048]{2,1,0:T(8,128)(2,1)} %copy-done.5, bf16[16,16,2048]{2,1,0:T(8,128)(2,1)} %collective-permute-done.3.refs_1_, f32[1024,128]{1,0:T(8,128)} %pad_maximum_fusion.3.refs_2_, f32[1024,128]{1,0:T(8,128)} %pad_maximum_fusion.4.refs_3_, ...), custom_call_target="tpu_custom_call" | custom-call | flops 2147483648 | bytes 7340032 | tf_op jit(solution)/shard_map/project/pallas_call | solution.py:121
  235.1 17.0 %attend_guest.3 = bf16[512,1152]{1,0:T(8,128)(2,1)} custom-call(s32[1]{0:T(128)} %get-tuple-element.131.count_ref, bf16[512,1024]{1,0:T(8,128)(2,1)} %project.9.q_ref, bf16[1,2,2048,1024]{3,2,1,0:T(8,128)(2,1)} %v_ref.3, bf16[1,2,2048,1024]{3,2,1,0:T(8,128)(2,1)} %v_ref.3), custom_call_target="tpu_custom_call" | custom-call | flops 17179869184 | bytes 10485760 | tf_op jit(solution)/shard_map/attend_guest/pallas_call | solution.py:330
  252.1 6.0 %all-to-all-start.6 = ((bf16[16,32,1152]{2,1,0:T(8,128)(2,1)}), bf16[16,32,1152]{2,1,0:T(8,128)(2,1)S(1)}, u32[]{:S(2)}, u32[]{:S(2)}) async-start(bf16[16,32,1152]{2,1,0:T(8,128)(2,1)} %bitcast.35), calls=%async_computation.6 | async-start | bytes 2359296 | tf_op jit(solution)/shard_map/all_to_all | solution.py:449
  259.7 24.3 %collective-permute-done.4 = bf16[512,1024]{1,0:T(8,128)(2,1)} collective-permute-done((bf16[512,1024]{1,0:T(8,128)(2,1)}, bf16[512,1024]{1,0:T(8,128)(2,1)}, u32[]{:S(2)}, u32[]{:S(2)}) %collective-permute-start.4) | collective-permute-done | bytes 1048608 | tf_op jit(solution)/shard_map/ppermute | solution.py:588
  285.0 8.3 %merge.3 = (bf16[512,1024]{1,0:T(8,128)(2,1)}, bf16[512,1024]{1,0:T(8,128)(2,1)}) custom-call(s32[16]{0:T(128)} %select_reduce_fusion.inverse_ref, s32[1]{0:T(128)} %bitcast.tp_ref, bf16[16,32,1152]{2,1,0:T(8,128)(2,1)} %copy-done.2, bf16[16,32,1152]{2,1,0:T(8,128)(2,1)} %copy-done.4, bf16[1024,2048]{1,0:T(8,128)(2,1)} %w_ref.3), custom_call_target="tpu_custom_call" | custom-call | flops 1073741824 | bytes 1048576 | tf_op jit(solution)/shard_map/merge/pallas_call | solution.py:425
  294.8 1.6 add_convert_fusion.1
  296.4 22.1 %collective-permute-done.5 = bf16[512,1024]{1,0:T(8,128)(2,1)S(1)} collective-permute-done((bf16[512,1024]{1,0:T(8,128)(2,1)}, bf16[512,1024]{1,0:T(8,128)(2,1)S(1)}, u32[]{:S(2)}, u32[]{:S(2)}) %collective-permute-start.5) | collective-permute-done | bytes 1048608 | tf_op jit(solution)/shard_map/ppermute | solution.py:588
  (66 shorter events, 23.1 us)
Async XLA Ops:
  5.3 7.5 %copy-start.12 = (s32[16]{0:T(128)S(1)}, s32[16]{0:T(128)}, u32[]{:S(2)}) copy-start(s32[16]{0:T(128)} %param.22) | copy-start | bytes 196
  5.3 7.5 %copy-start.13 = (s32[16]{0:T(128)S(1)}, s32[16]{0:T(128)}, u32[]{:S(2)}) copy-start(s32[16]{0:T(128)} %param.21) | copy-start | bytes 196
  5.3 30.4 %all-to-all-start = ((bf16[16,16,2048]{2,1,0:T(8,128)(2,1)}), bf16[16,16,2048]{2,1,0:T(8,128)(2,1)S(1)}, u32[]{:S(2)}, u32[]{:S(2)}) async-start(bf16[16,16,2048]{2,1,0:T(8,128)(2,1)} %get-tuple-element.61), calls=%async_computation | async-start | bytes 2097152 | tf_op jit(solution)/shard_map/all_to_all | solution.py:449
  16.4 4.7 %copy-start.11 = (s32[1,256]{1,0:T(1,128)S(1)}, s32[1,256]{1,0:T(1,128)}, u32[]{:S(2)}) copy-start(s32[1,256]{1,0:T(1,128)} %index_ref.1) | copy-start | bytes 3076
  22.5 3.0 copy-start
  35.7 19.4 %copy-start.9 = (bf16[16,16,2048]{2,1,0:T(8,128)(2,1)}, bf16[16,16,2048]{2,1,0:T(8,128)(2,1)S(1)}, u32[]{:S(2)}) copy-start(bf16[16,16,2048]{2,1,0:T(8,128)(2,1)S(1)} %all-to-all-done.refs_0_) | copy-start | bytes 3145732
  35.7 32.4 %all-to-all-start.1 = ((bf16[16,16,2048]{2,1,0:T(8,128)(2,1)}), bf16[16,16,2048]{2,1,0:T(8,128)(2,1)S(1)}, u32[]{:S(2)}, u32[]{:S(2)}) async-start(bf16[16,16,2048]{2,1,0:T(8,128)(2,1)} %get-tuple-element.65), calls=%async_computation.1 | async-start | bytes 2097152 | tf_op jit(solution)/shard_map/all_to_all | solution.py:449
  42.6 25.5 %collective-permute-start = (bf16[16,16,2048]{2,1,0:T(8,128)(2,1)S(1)}, bf16[16,16,2048]{2,1,0:T(8,128)(2,1)S(1)}, u32[]{:S(2)}, u32[]{:S(2)}) collective-permute-start(bf16[16,16,2048]{2,1,0:T(8,128)(2,1)S(1)} %all-to-all-done.refs_0_), channel_id=1, source_target_pairs={{0,1},{1,0},{2,3},{3,2},{4,5},{5,4},{6,7},{7,6},{8,9},{9,8},{10,11... | collective-permute-start | bytes 3145736 | tf_op jit(solution)/shard_map/ppermute | solution.py:500
  68.1 1.0 copy-start.15
  68.1 1.3 copy-start.10
  69.4 46.9 %all-to-all-start.2 = ((bf16[16,32,2048]{2,1,0:T(8,128)(2,1)}), bf16[16,32,2048]{2,1,0:T(8,128)(2,1)S(1)}, u32[]{:S(2)}, u32[]{:S(2)}) async-start(bf16[16,32,2048]{2,1,0:T(8,128)(2,1)} %get-tuple-element.70), calls=%async_computation.2 | async-start | bytes 4194304 | tf_op jit(solution)/shard_map/all_to_all | solution.py:449
  75.2 25.8 %collective-permute-start.1 = (bf16[16,16,2048]{2,1,0:T(8,128)(2,1)}, bf16[16,16,2048]{2,1,0:T(8,128)(2,1)S(1)}, u32[]{:S(2)}, u32[]{:S(2)}) collective-permute-start(bf16[16,16,2048]{2,1,0:T(8,128)(2,1)} %copy-done.10), channel_id=1, source_target_pairs={{0,1},{1,0},{2,3},{3,2},{4,5},{5,4},{6,7},{7,6},{8,9},{9,8},{10,11... | collective-permute-start | bytes 3145736 | tf_op jit(solution)/shard_map/ppermute | solution.py:500
  100.9 1.0 copy-start.16
  117.4 69.4 %copy-start.5 = (bf16[16,16,2048]{2,1,0:T(8,128)(2,1)}, bf16[16,16,2048]{2,1,0:T(8,128)(2,1)S(1)}, u32[]{:S(2)}) copy-start(bf16[16,16,2048]{2,1,0:T(8,128)(2,1)S(1)} %get-tuple-element.102.refs_0_) | copy-start | bytes 3145732
  117.4 26.0 %collective-permute-start.2 = (bf16[16,16,2048]{2,1,0:T(8,128)(2,1)}, bf16[16,16,2048]{2,1,0:T(8,128)(2,1)S(1)}, u32[]{:S(2)}, u32[]{:S(2)}) collective-permute-start(bf16[16,16,2048]{2,1,0:T(8,128)(2,1)} %get-tuple-element.93.refs_0_), channel_id=1, source_target_pairs={{0,1},{1,0},{2,3},{3,2},{4,5},{5,4},{6,7},{7,6},{8,9},{9,8},{10,11... | collective-permute-start | bytes 3145736 | tf_op jit(solution)/shard_map/ppermute | solution.py:500
  143.5 10.8 %copy-start.8 = (bf16[16,16,2048]{2,1,0:T(8,128)(2,1)}, bf16[16,16,2048]{2,1,0:T(8,128)(2,1)S(1)}, u32[]{:S(2)}) copy-start(bf16[16,16,2048]{2,1,0:T(8,128)(2,1)S(1)} %collective-permute-done.2.refs_1_) | copy-start | bytes 3145732
  143.5 35.9 %all-to-all-start.3 = ((bf16[16,32,1152]{2,1,0:T(8,128)(2,1)}), bf16[16,32,1152]{2,1,0:T(8,128)(2,1)S(1)}, u32[]{:S(2)}, u32[]{:S(2)}) async-start(bf16[16,32,1152]{2,1,0:T(8,128)(2,1)} %bitcast.36), calls=%async_computation.3 | async-start | bytes 2359296 | tf_op jit(solution)/shard_map/all_to_all | solution.py:449
  179.4 31.3 %copy-start.1 = (bf16[16,32,1152]{2,1,0:T(8,128)(2,1)}, bf16[16,32,1152]{2,1,0:T(8,128)(2,1)S(1)}, u32[]{:S(2)}) copy-start(bf16[16,32,1152]{2,1,0:T(8,128)(2,1)S(1)} %all-to-all-done.3.own_ref) | copy-start | bytes 3538948
  179.4 33.2 %all-to-all-start.4 = ((bf16[16,32,1152]{2,1,0:T(8,128)(2,1)}), bf16[16,32,1152]{2,1,0:T(8,128)(2,1)S(1)}, u32[]{:S(2)}, u32[]{:S(2)}) async-start(bf16[16,32,1152]{2,1,0:T(8,128)(2,1)} %bitcast.34), calls=%async_computation.4 | async-start | bytes 2359296 | tf_op jit(solution)/shard_map/all_to_all | solution.py:449
  186.9 25.7 %collective-permute-start.3 = (bf16[16,16,2048]{2,1,0:T(8,128)(2,1)S(1)}, bf16[16,16,2048]{2,1,0:T(8,128)(2,1)}, u32[]{:S(2)}, u32[]{:S(2)}) collective-permute-start(bf16[16,16,2048]{2,1,0:T(8,128)(2,1)S(1)} %get-tuple-element.102.refs_0_), channel_id=1, source_target_pairs={{0,1},{1,0},{2,3},{3,2},{4,5},{5,4},{6,7},{7,6},{8,9},{9,8},{10,11... | collective-permute-start | bytes 3145736 | tf_op jit(solution)/shard_map/ppermute | solution.py:500
  210.6 8.9 %copy-start.14 = (s32[16]{0:T(128)S(1)}, s32[16]{0:T(128)}, u32[]{:S(2)}) copy-start(s32[16]{0:T(128)} %order_ref.1) | copy-start | bytes 196
  212.5 7.6 %copy-start.3 = (bf16[16,32,1152]{2,1,0:T(8,128)(2,1)}, bf16[16,32,1152]{2,1,0:T(8,128)(2,1)S(1)}, u32[]{:S(2)}) copy-start(bf16[16,32,1152]{2,1,0:T(8,128)(2,1)S(1)} %all-to-all-done.4.guest_ref) | copy-start | bytes 3538948
  212.5 39.5 %all-to-all-start.5 = ((bf16[16,32,1152]{2,1,0:T(8,128)(2,1)}), bf16[16,32,1152]{2,1,0:T(8,128)(2,1)S(1)}, u32[]{:S(2)}, u32[]{:S(2)}) async-start(bf16[16,32,1152]{2,1,0:T(8,128)(2,1)} %bitcast.33), calls=%async_computation.5 | async-start | bytes 2359296 | tf_op jit(solution)/shard_map/all_to_all | solution.py:449
  252.1 31.9 %copy-start.2 = (bf16[16,32,1152]{2,1,0:T(8,128)(2,1)}, bf16[16,32,1152]{2,1,0:T(8,128)(2,1)S(1)}, u32[]{:S(2)}) copy-start(bf16[16,32,1152]{2,1,0:T(8,128)(2,1)S(1)} %all-to-all-done.5.own_ref) | copy-start | bytes 3538948
  252.1 31.9 %all-to-all-start.6 = ((bf16[16,32,1152]{2,1,0:T(8,128)(2,1)}), bf16[16,32,1152]{2,1,0:T(8,128)(2,1)S(1)}, u32[]{:S(2)}, u32[]{:S(2)}) async-start(bf16[16,32,1152]{2,1,0:T(8,128)(2,1)} %bitcast.35), calls=%async_computation.6 | async-start | bytes 2359296 | tf_op jit(solution)/shard_map/all_to_all | solution.py:449
  258.1 36.7 %copy-start.6 = (bf16[512,1024]{1,0:T(8,128)(2,1)S(1)}, bf16[512,1024]{1,0:T(8,128)(2,1)}, u32[]{:S(2)}) copy-start(bf16[512,1024]{1,0:T(8,128)(2,1)} %get-tuple-element.111) | copy-start | bytes 3145732
  258.1 25.9 %collective-permute-start.4 = (bf16[512,1024]{1,0:T(8,128)(2,1)}, bf16[512,1024]{1,0:T(8,128)(2,1)}, u32[]{:S(2)}, u32[]{:S(2)}) collective-permute-start(bf16[512,1024]{1,0:T(8,128)(2,1)} %get-tuple-element.110), channel_id=1, source_target_pairs={{0,1},{1,0},{2,3},{3,2},{4,5},{5,4},{6,7},{7,6},{8,9},{9,8},{10,11... | collective-permute-start | bytes 3145736 | tf_op jit(solution)/shard_map/ppermute | solution.py:588
  283.9 1.0 copy-start.4
  293.3 25.3 %copy-start.7 = (bf16[512,1024]{1,0:T(8,128)(2,1)S(1)}, bf16[512,1024]{1,0:T(8,128)(2,1)}, u32[]{:S(2)}) copy-start(bf16[512,1024]{1,0:T(8,128)(2,1)} %get-tuple-element.115) | copy-start | bytes 3145732
  293.3 25.3 %collective-permute-start.5 = (bf16[512,1024]{1,0:T(8,128)(2,1)}, bf16[512,1024]{1,0:T(8,128)(2,1)S(1)}, u32[]{:S(2)}, u32[]{:S(2)}) collective-permute-start(bf16[512,1024]{1,0:T(8,128)(2,1)} %get-tuple-element.116), channel_id=1, source_target_pairs={{0,1},{1,0},{2,3},{3,2},{4,5},{5,4},{6,7},{7,6},{8,9},{9,8},{10,11... | collective-permute-start | bytes 3145736 | tf_op jit(solution)/shard_map/ppermute | solution.py:588
